TPU v7x, 512 devices: a whole 4x4x16 slice. The times are simulated.
512 devices in a mesh: fsdp: 128 (over z, y, core), rep: 4 (over x).
Axes of the slice: x: 4, y: 4, z: 16, core: 2. Of those that a mesh axis runs over, the one named last changes fastest.
Arguments:
- grad: float32 [128, 512, 512], P(None, 'fsdp'), may hold values from -6 to 6
- left_factor: float32 [256, 512, 512], P('fsdp', 'rep')
- right_factor: float32 [256, 512, 512], P('fsdp', 'rep')
- left_root: float32 [256, 512, 512], P('fsdp', 'rep'), as said below
- right_root: float32 [256, 512, 512], P('fsdp', 'rep'), as said below
- owner_table: int32 [128], replicated, may hold values from 0 to 127, as said below
Outputs:
- new_left: float32 [256, 512, 512], P('fsdp', 'rep')
- new_right: float32 [256, 512, 512], P('fsdp', 'rep')
- direction: float32 [128, 512, 512], P(None, 'fsdp', 'rep')
Inputs may be any that keep to these rules, and one draw needn't show every extreme that they name: `owner_table`: each fsdp index owns at most 2 blocks, and some index owns exactly 2. Every matrix right_root[i] is symmetric. Every matrix left_root[i] is symmetric.
All inputs are finite; a program needn't handle non-finite values.
Results may differ from a plain program's by a relative error of at most 0.00007.
Values sent between devices are 32-bit elements; how exact they have to be, the bound alone decides.
A program may use at most 64 MiB of HBM per device.

v0:
```python
import jax
import jax.numpy as jnp
from jax import lax
from jax.sharding import PartitionSpec as P

moment_decay = 0.9


def body(grad, left_factor, right_factor, left_root, right_root, owner_table):
    owner_count = lax.axis_size("fsdp")
    owner_index = lax.axis_index("fsdp")
    rep_index = lax.axis_index("rep")
    block_count, row_count, matrix_order = grad.shape
    slots = left_factor.shape[0]
    quarter = left_factor.shape[1]
    highest = lax.Precision.HIGHEST
    weight = (1.0 - moment_decay) / matrix_order
    numbers = jnp.arange(block_count, dtype=jnp.int32)
    same_owner = owner_table[:, None] == owner_table[None, :]
    before = numbers[None, :] < numbers[:, None]
    slot_of = jnp.sum((same_owner & before).astype(jnp.int32), axis=1)
    home = owner_table * slots + slot_of
    all_homes = jnp.arange(owner_count * slots, dtype=jnp.int32)
    home_match = home[None, :] == all_homes[:, None]
    filled = jnp.any(home_match, axis=1)
    source = jnp.sum(jnp.where(home_match, numbers[None, :], 0), axis=1)
    outgoing = jnp.where(filled[:, None, None], grad[source], 0.0)
    blocks = lax.all_to_all(outgoing, "fsdp", split_axis=0, concat_axis=1, tiled=True)
    live_slots = lax.dynamic_slice_in_dim(filled, owner_index * slots, slots)
    band_rows = lax.dynamic_slice_in_dim(blocks, rep_index * quarter, quarter, 1)
    band_cols = lax.dynamic_slice_in_dim(blocks, rep_index * quarter, quarter, 2)
    left_term = jnp.einsum("sik,sjk->sij", band_rows, blocks, precision=highest)
    right_term = jnp.einsum("ski,skj->sij", band_cols, blocks, precision=highest)
    left_next = moment_decay * left_factor + weight * left_term
    right_next = moment_decay * right_factor + weight * right_term
    left_out = jnp.where(live_slots[:, None, None], left_next, left_factor)
    right_out = jnp.where(live_slots[:, None, None], right_next, right_factor)
    turned = jnp.einsum("skj,sij->ski", blocks, right_root, precision=highest)
    steered = jnp.einsum(
        "sik,skj->sij",
        lax.all_gather(left_root, "rep", axis=1, tiled=True),
        turned,
        precision=highest,
    )
    returned = lax.all_to_all(steered, "fsdp", split_axis=1, concat_axis=0, tiled=True)
    direction = returned[home]
    return (left_out, right_out, direction)


def solution(mesh):
    placed = (
        P(None, "fsdp", None),
        P("fsdp", "rep", None),
        P("fsdp", "rep", None),
        P("fsdp", "rep", None),
        P("fsdp", "rep", None),
        P(),
    )
    return jax.shard_map(
        body,
        mesh=mesh,
        in_specs=placed,
        out_specs=(P("fsdp", "rep", None), P("fsdp", "rep", None), P(None, "fsdp", "rep")),
        check_vma=False,
    )
```

profile of v0, /device:TPU:1, one launch (start us, length us, event | category | flops | bytes accessed | tf_op | source)
XLA Modules:
  0.0 196.1 jit_solution(13935081520163454703)
XLA Ops:
  7.2 0.9 convert_reduce_fusion
  8.1 0.7 compare_select_fusion.1
  8.8 0.1 select_reduce_fusion
  8.9 0.1 fusion.6
  9.0 1.9 gather_fusion
  10.9 2.0 %broadcast_select_fusion = f32[256,4,512]{2,1,0:T(4,128)} fusion(f32[256,4,512]{2,1,0:T(4,128)S(1)} %gather_fusion, pred[256]{0:T(512)(128)(4,1)S(1)} %fusion.6), kind=kLoop, calls=%fused_computation.10 | loop fusion | flops 524288 | bytes 4194560 | tf_op jit(solution)/shard_map/jit(_where)/select_n | solution.py:27
  12.9 20.6 %all-to-all-start = ((f32[256,4,512]{2,1,0:T(4,128)}), f32[256,4,512]{2,1,0:T(4,128)S(1)}, u32[]{:S(2)}, u32[]{:S(2)}) async-start(f32[256,4,512]{2,1,0:T(4,128)} %broadcast_select_fusion), calls=%async_computation | async-start | bytes 4194304 | tf_op jit(solution)/shard_map/all_to_all | solution.py:28
  33.5 0.0 all-gather.2.cloned.1.call-start
  33.6 0.7 all-gather.2.cloned.1.call-update
  34.3 96.1 %all-to-all-done = f32[256,4,512]{2,1,0:T(4,128)S(1)} async-done(((f32[256,4,512]{2,1,0:T(4,128)}), f32[256,4,512]{2,1,0:T(4,128)S(1)}, u32[]{:S(2)}, u32[]{:S(2)}) %all-to-all-start) | async-done | bytes 2097184 | tf_op jit(solution)/shard_map/all_to_all | solution.py:28
  130.4 1.7 copy.33
  132.1 2.0 %all_to_all.29 = f32[2,512,512]{2,1,0:T(8,128)S(1)} reshape(f32[2,128,4,512]{3,2,1,0:T(4,128)} %bitcast.19) | data formatting | bytes 4194304 | tf_op jit(solution)/shard_map/all_to_all | solution.py:28
  134.0 4.1 %fusion.10 = f32[2,512,128]{1,2,0:T(8,128)} fusion(f32[2,512,512]{2,1,0:T(8,128)S(1)} %all_to_all.29, f32[2,128,512]{2,1,0:T(8,128)} %param.10), kind=kOutput, calls=%fused_computation.26 | convolution fusion | flops 805306368 | bytes 3145728 | tf_op jit(solution)/shard_map/skj,sij->ski/dot_general | solution.py:38
  138.1 4.8 %convolution_bitcast_fusion = f32[2,512,128]{1,2,0:T(8,128)} fusion(f32[2,512,128]{1,2,0:T(8,128)} %fusion.10, f32[2,512,512]{2,1,0:T(8,128)} %all-gather.2.cloned.1.call-done), kind=kOutput, calls=%fused_computation.3 | convolution fusion | flops 805306368 | bytes 3145728 | tf_op jit(solution)/shard_map/sik,skj->sij/dot_general | solution.py:39
  142.9 2.0 %copy.26 = f32[2,512,128]{2,0,1:T(2,128)} copy(f32[2,512,128]{1,2,0:T(8,128)} %convolution_bitcast_fusion) | data formatting | bytes 1048576 | tf_op jit(solution)/shard_map/sik,skj->sij/dot_general | solution.py:39
  145.0 10.5 %all-to-all-start.1 = ((f32[2,512,128]{2,0,1:T(2,128)}), f32[2,512,128]{2,0,1:T(2,128)}, u32[]{:S(2)}, u32[]{:S(2)}) async-start(f32[2,512,128]{2,0,1:T(2,128)} %copy.26), calls=%async_computation.1 | async-start | bytes 1048576 | tf_op jit(solution)/shard_map/all_to_all | solution.py:45
  155.5 0.1 dynamic_slice.9
  155.6 4.2 %fusion.3 = f32[2,128,512]{2,1,0:T(8,128)} fusion(f32[2,128,512]{2,1,0:T(8,128)} %param.7, f32[2,512,512]{2,1,0:T(8,128)S(1)} %all_to_all.29, s32[]{:T(128)S(6)} %select_n.39, pred[2]{0:T(512)(128)(4,1)S(1)} %dynamic_slice.9), kind=kOutput, calls=%fused_computation.9 | convolution fusion | flops 805830656 | bytes 3670532 | tf_op jit(solution)/shard_map/sik,sjk->sij/dot_general | solution.py:32
  159.8 2.2 %fusion.1 = f32[2,128,512]{2,1,0:T(8,128)} fusion(f32[2,128,512]{2,1,0:T(8,128)S(1)} %copy-done.1, f32[2,512,512]{2,1,0:T(8,128)S(1)} %all_to_all.29, s32[]{:T(128)S(6)} %select_n.39, pred[2]{0:T(512)(128)(4,1)S(1)} %dynamic_slice.9), kind=kOutput, calls=%fused_computation.6 | convolution fusion | flops 805830656 | bytes 3670532 | tf_op jit(solution)/shard_map/ski,skj->sij/dot_general | solution.py:33
  162.0 24.0 %all-to-all-done.1 = f32[2,512,128]{2,0,1:T(2,128)} async-done(((f32[2,512,128]{2,0,1:T(2,128)}), f32[2,512,128]{2,0,1:T(2,128)}, u32[]{:S(2)}, u32[]{:S(2)}) %all-to-all-start.1) | async-done | bytes 524320 | tf_op jit(solution)/shard_map/all_to_all | solution.py:45
  186.0 1.1 copy.27
  187.1 0.4 copy.28
  187.5 0.3 copy.29
  187.8 1.4 gather_fusion.1
  (8 shorter events, 0.0 us)
Async XLA Ops:
  7.2 1.9 copy-start
  12.9 117.4 %all-to-all-start = ((f32[256,4,512]{2,1,0:T(4,128)}), f32[256,4,512]{2,1,0:T(4,128)S(1)}, u32[]{:S(2)}, u32[]{:S(2)}) async-start(f32[256,4,512]{2,1,0:T(4,128)} %broadcast_select_fusion), calls=%async_computation | async-start | bytes 4194304 | tf_op jit(solution)/shard_map/all_to_all | solution.py:28
  33.5 104.6 %all-gather.2.cloned.1.call-start = ((), (), s32[]{:S(2)}) async-start(), calls=%async_computation.2 | async-start | bytes 2621440 | tf_op jit(solution)/shard_map/all_gather | solution.py:41
  145.0 41.0 %all-to-all-start.1 = ((f32[2,512,128]{2,0,1:T(2,128)}), f32[2,512,128]{2,0,1:T(2,128)}, u32[]{:S(2)}, u32[]{:S(2)}) async-start(f32[2,512,128]{2,0,1:T(2,128)} %copy.26), calls=%async_computation.1 | async-start | bytes 1048576 | tf_op jit(solution)/shard_map/all_to_all | solution.py:45
  155.6 4.2 %copy-start.1 = (f32[2,128,512]{2,1,0:T(8,128)S(1)}, f32[2,128,512]{2,1,0:T(8,128)}, u32[]{:S(2)}) copy-start(f32[2,128,512]{2,1,0:T(8,128)} %param.8) | copy-start | bytes 1572868
Sparse Core Ops, SparseCore 0:
  36.5 39.3 all-gather.1
where the time goes:
time: 198 us; the launch traced here: 196 us
  waiting for transfers between devices  121 us (61%)
  starting transfers between devices  31.1 us (16%)
  matrix products  15.2 us (8%)
  between operations  14.1 us (7%)
  local copies, waits for them, and re-layouts  10.9 us (6%)
  other arithmetic  3.88 us (2%)
    all_to_all x1, waiting for transfers between devices, body(): lax.all_to_all(outgoing, 'fsdp', split_axis=0, concat_axis=1, tiled=True)  96.1 us
    all_to_all x1, waiting for transfers between devices, body(): lax.all_to_all(steered, 'fsdp', split_axis=1, concat_axis=0, tiled=True)  24 us
    all_to_all x1, starting transfers between devices, body(): lax.all_to_all(outgoing, 'fsdp', split_axis=0, concat_axis=1, tiled=True)  20.6 us
    all_to_all x1, starting transfers between devices, body(): lax.all_to_all(steered, 'fsdp', split_axis=1, concat_axis=0, tiled=True)  10.5 us
    dot_general x1, matrix products, body(): jnp.einsum('sik,skj->sij', lax.all_gather(left_root, 'rep', axis=1, tiled...  4.8 us
    dot_general x1, matrix products, body(): left_term = jnp.einsum('sik,sjk->sij', band_rows, blocks, precision=highest)  4.15 us
    dot_general x1, matrix products, body(): turned = jnp.einsum('skj,sij->ski', blocks, right_root, precision=highest)  4.1 us
  transfers between devices with their start and end apart: 3, of which 2 were waited for; matrix products, arithmetic and copies ran while one was open for 6% of the time, Pallas kernels for 0%

commit v1 on v0

v1 whole, which is shorter than its diff:
```python
import functools

import jax
import jax.numpy as jnp
from jax import lax
from jax.experimental import pallas as pl
from jax.experimental.pallas import tpu as pltpu
from jax.sharding import PartitionSpec as P

moment_decay = 0.9
MESH = pl.DeviceIdType.MESH
bf16 = jnp.bfloat16
f32 = jnp.float32

NZ, NS, NX = 16, 8, 4
Z_IN, S_IN, X_A, X_B, X_FA, X_FB, S_OUT, Z_OUT, L_A, L_B, L_FA, L_FB = range(12)
C_G, C_R, C_LF, C_RF = range(4)


def split(x):
    hi = x.astype(bf16)
    return hi, (x - hi.astype(f32)).astype(bf16)


def dot3(a, b, dims):
    def one(p, q):
        return lax.dot_general(p, q, (dims, ((), ())), preferred_element_type=f32)

    return one(a[0], b[0]) + (one(a[0], b[1]) + one(a[1], b[0]))


def kernel(
    owner_ref, table_ref, grad_ref, lf_ref, rf_ref, lroot_ref, rroot_ref, live_ref,
    left_out, right_out, dir_out,
    gq, send, zin, gbuf, band, ghi, glo, lbuf, rr, lf, rf, dbuf, pout, rbuf,
    send_sem, recv_sem, loc_sem, in_sem,
):
    me, r = lax.axis_index("fsdp"), lax.axis_index("rep")
    z, s = lax.div(me, NS), lax.rem(me, NS)
    xa, xb = lax.rem(r + 1, NX), lax.rem(r + 3, NX)
    xc = lax.rem(r + 2, NX)

    def remote(src, dst, kind, k, dev):
        return pltpu.make_async_remote_copy(
            src_ref=src, dst_ref=dst, send_sem=send_sem.at[kind, k], recv_sem=recv_sem.at[kind, k],
            device_id=dev, device_id_type=MESH,
        )

    def wait_bytes(ref, sem):
        pltpu.make_async_copy(ref, ref, sem).wait()

    def zdev(d):
        zz = lax.rem(z + d, NZ)
        return zz, (zz * NS + s, r)

    def sdev(d):
        ss = lax.rem(s + d, NS)
        return ss, (z * NS + ss, r)

    def load(src, dst, i):
        c = pltpu.make_async_copy(src, dst, in_sem.at[i])
        c.start()
        return c

    cols = pl.ds(pl.multiple_of(r * 128, 128), 128)
    in_g = load(grad_ref.at[:, :, cols], gq, C_G)
    in_r = load(rroot_ref, rr, C_R)
    in_lf = load(lf_ref, lf, C_LF)
    in_rf = load(rf_ref, rf, C_RF)

    barrier = pltpu.get_barrier_semaphore()

    @pl.loop(1, NZ)
    def _(d):
        pl.semaphore_signal(barrier, inc=1, device_id=zdev(d)[1], device_id_type=MESH)

    @pl.loop(1, NS)
    def _(d):
        pl.semaphore_signal(barrier, inc=1, device_id=sdev(d)[1], device_id_type=MESH)

    for x in (xa, xb):
        pl.semaphore_signal(barrier, inc=1, device_id=(me, x), device_id_type=MESH)

    in_g.wait()

    def pack(k):
        @pl.loop(0, 128, unroll=8)
        def _(o):
            send[k, o] = gq[table_ref[k, o]]

    pack(0)
    pl.semaphore_wait(barrier, NZ - 1 + NS - 1 + 2)

    def z_in(k):
        @pl.loop(1, NZ)
        def _(d):
            zz, dev = zdev(d)
            remote(send.at[k, pl.ds(zz * NS, NS)], zin.at[k, z], Z_IN, k, dev).start()

        c = pltpu.make_async_copy(send.at[k, pl.ds(z * NS, NS)], zin.at[k, z], loc_sem.at[0, k])
        c.start()
        return c

    def x_pair(own, src, ka, kb, k):
        remote(src, own, ka, k, (me, xa)).start()
        remote(src, own, kb, k, (me, xb)).start()

    own_z = [None, None]
    own_z[0] = z_in(0)
    loc_l = []
    for k in range(2):
        x_pair(lbuf.at[r, k], lroot_ref.at[k], L_A, L_B, k)
        c = pltpu.make_async_copy(lroot_ref.at[k], lbuf.at[r, k], loc_sem.at[1, k])
        c.start()
        loc_l.append(c)
    pack(1)
    own_z[1] = z_in(1)

    def l_forward(k):
        wait_bytes(lbuf.at[xb, k], recv_sem.at[L_A, k])
        h = lbuf.at[xb, k, pl.ds(0, 64)]
        remote(h, h, L_FA, k, (me, xa)).start()
        wait_bytes(lbuf.at[xa, k], recv_sem.at[L_B, k])
        h = lbuf.at[xa, k, pl.ds(64, 64)]
        remote(h, h, L_FB, k, (me, xb)).start()

    def s_in(k):
        wait_bytes(zin.at[k, pl.ds(0, NZ - 1)], recv_sem.at[Z_IN, k])
        own_z[k].wait()

        @pl.loop(1, NS)
        def _(d):
            ss, dev = sdev(d)
            remote(zin.at[k, :, ss], gbuf.at[k, r, :, s], S_IN, k, dev).start()

        c = pltpu.make_async_copy(zin.at[k, :, s], gbuf.at[k, r, :, s], loc_sem.at[2, k])
        c.start()
        return c

    def x_start(k, own):
        wait_bytes(gbuf.at[k, r, :, pl.ds(0, NS - 1)], recv_sem.at[S_IN, k])
        own.wait()
        g = gbuf.at[k, r]
        x_pair(g, g, X_A, X_B, k)

    def take(k, q):
        @pl.loop(0, NZ)
        def _(zz):
            base = pl.multiple_of(zz * 32, 32)
            for ss in range(NS):
                band[pl.ds(base + ss * 4, 4), :] = gbuf[k, q, zz, ss]

        hi, lo = split(band[...])
        at = pl.ds(pl.multiple_of(q * 128, 128), 128)
        ghi[k, :, at] = hi
        glo[k, :, at] = lo

    def x_forward(k):
        wait_bytes(gbuf.at[k, xb], recv_sem.at[X_A, k])
        h = gbuf.at[k, xb, pl.ds(0, 8)]
        remote(h, h, X_FA, k, (me, xa)).start()
        wait_bytes(gbuf.at[k, xa], recv_sem.at[X_B, k])
        h = gbuf.at[k, xa, pl.ds(8, 8)]
        remote(h, h, X_FB, k, (me, xb)).start()

    def x_end(k):
        wait_bytes(gbuf.at[k, xc, pl.ds(0, 8)], recv_sem.at[X_FA, k])
        wait_bytes(gbuf.at[k, xc, pl.ds(8, 8)], recv_sem.at[X_FB, k])

    def steer(k):
        turned = dot3((ghi[k], glo[k]), split(rr[k]), ((1,), (1,)))
        t = split(turned)
        for q in range(NX):
            part = dot3(split(lbuf[q, k]), t, ((1,), (0,)))
            band[pl.ds(q * 128, 128), :] = part

        @pl.loop(0, NZ)
        def _(zz):
            base = pl.multiple_of(zz * 32, 32)
            for ss in range(NS):
                dbuf[k, zz, ss] = band[pl.ds(base + ss * 4, 4), :]

    def s_out(k):
        @pl.loop(1, NS)
        def _(d):
            ss, dev = sdev(d)
            remote(dbuf.at[k, :, ss], pout.at[k, :, s], S_OUT, k, dev).start()

        c = pltpu.make_async_copy(dbuf.at[k, :, s], pout.at[k, :, s], loc_sem.at[3, k])
        c.start()
        return c

    def z_out(k, own):
        wait_bytes(pout.at[k, :, pl.ds(0, NS - 1)], recv_sem.at[S_OUT, k])
        own.wait()

        @pl.loop(1, NZ)
        def _(d):
            zz, dev = zdev(d)
            remote(pout.at[k, zz], rbuf.at[k, z], Z_OUT, k, dev).start()

        c = pltpu.make_async_copy(pout.at[k, z], rbuf.at[k, z], loc_sem.at[4, k])
        c.start()
        return c

    weight = (1.0 - moment_decay) / 512
    rows = pl.ds(pl.multiple_of(r * 128, 128), 128)

    def stats(k):
        live = live_ref[k][:1, :1] > 0
        g = (ghi[k], glo[k])
        term = dot3((ghi[k, rows, :], glo[k, rows, :]), g, ((1,), (1,)))
        old = lf[k]
        left_out[k] = jnp.where(live, moment_decay * old + weight * term, old)
        term = dot3((ghi[k, :, rows], glo[k, :, rows]), g, ((0,), (0,)))
        old = rf[k]
        right_out[k] = jnp.where(live, moment_decay * old + weight * term, old)

    own0 = s_in(0)
    l_forward(0)
    x_start(0, own0)
    take(0, r)
    l_forward(1)
    own1 = s_in(1)
    x_forward(0)
    take(0, xb)
    take(0, xa)
    x_start(1, own1)
    take(1, r)
    in_r.wait()
    for k in range(2):
        loc_l[k].wait()
    for k in range(2):
        wait_bytes(lbuf.at[xc, k, pl.ds(0, 64)], recv_sem.at[L_FA, k])
        wait_bytes(lbuf.at[xc, k, pl.ds(64, 64)], recv_sem.at[L_FB, k])
    x_end(0)
    take(0, xc)
    steer(0)
    out0 = s_out(0)
    x_forward(1)
    in_lf.wait()
    in_rf.wait()
    fin0 = z_out(0, out0)
    take(1, xb)
    take(1, xa)
    x_end(1)
    take(1, xc)
    steer(1)
    out1 = s_out(1)
    stats(0)
    fin1 = z_out(1, out1)
    stats(1)
    fins = [fin0, fin1]
    for k in range(2):
        wait_bytes(rbuf.at[k, pl.ds(0, NZ - 1)], recv_sem.at[Z_OUT, k])
        fins[k].wait()

    @pl.loop(0, 128, unroll=8)
    def _(b):
        o = owner_ref[b]
        k = jnp.where(table_ref[0, o] == b, 0, 1)
        dir_out[b] = rbuf[k, lax.div(o, NS), lax.rem(o, NS)]

    for k in range(2):
        wait_bytes(zin.at[k, pl.ds(0, NZ - 1)], send_sem.at[Z_IN, k])
        wait_bytes(gbuf.at[k, r, :, pl.ds(0, NS - 1)], send_sem.at[S_IN, k])
        for kind in (X_A, X_B):
            wait_bytes(gbuf.at[k, r], send_sem.at[kind, k])
        for kind in (X_FA, X_FB):
            wait_bytes(gbuf.at[k, r, pl.ds(0, 8)], send_sem.at[kind, k])
        for kind in (L_A, L_B):
            wait_bytes(lbuf.at[r, k], send_sem.at[kind, k])
        for kind in (L_FA, L_FB):
            wait_bytes(lbuf.at[r, k, pl.ds(0, 64)], send_sem.at[kind, k])
        wait_bytes(pout.at[k, :, pl.ds(0, NS - 1)], send_sem.at[S_OUT, k])
        wait_bytes(rbuf.at[k, pl.ds(0, NZ - 1)], send_sem.at[Z_OUT, k])


def body(grad, left_factor, right_factor, left_root, right_root, owner_table):
    numbers = jnp.arange(128, dtype=jnp.int32)
    match = owner_table[None, :] == numbers[:, None]
    first = jnp.min(jnp.where(match, numbers[None, :], 128), axis=1)
    last = jnp.max(jnp.where(match, numbers[None, :], -1), axis=1)
    table = jnp.stack([jnp.minimum(first, 127), jnp.maximum(last, 0)])
    me = lax.axis_index("fsdp")
    mine = jnp.stack([lax.dynamic_index_in_dim(first, me, 0, False), lax.dynamic_index_in_dim(last, me, 0, False)])
    live = jnp.stack([mine[0] < 128, mine[1] > mine[0]])
    live = jnp.broadcast_to(live.astype(jnp.int32)[:, None, None], (2, 8, 128))

    any_spec = pl.BlockSpec(memory_space=pl.ANY)
    vmem = pl.BlockSpec(memory_space=pltpu.VMEM)
    smem = pl.BlockSpec(memory_space=pltpu.SMEM)
    piece = (NZ, NS, 4, 128)
    return pl.pallas_call(
        kernel,
        out_shape=(
            jax.ShapeDtypeStruct((2, 128, 512), f32),
            jax.ShapeDtypeStruct((2, 128, 512), f32),
            jax.ShapeDtypeStruct((128, 4, 128), f32),
        ),
        in_specs=[smem, smem] + [any_spec] * 5 + [vmem],
        out_specs=(vmem, vmem, vmem),
        scratch_shapes=[
            pltpu.VMEM((128, 4, 128), f32),
            pltpu.VMEM((2, 128, 4, 128), f32),
            pltpu.VMEM((2,) + piece, f32),
            pltpu.VMEM((2, NX) + piece, f32),
            pltpu.VMEM((512, 128), f32),
            pltpu.VMEM((2, 512, 512), bf16),
            pltpu.VMEM((2, 512, 512), bf16),
            pltpu.VMEM((NX, 2, 128, 512), f32),
            pltpu.VMEM((2, 128, 512), f32),
            pltpu.VMEM((2, 128, 512), f32),
            pltpu.VMEM((2, 128, 512), f32),
            pltpu.VMEM((2,) + piece, f32),
            pltpu.VMEM((2,) + piece, f32),
            pltpu.VMEM((2,) + piece, f32),
            pltpu.SemaphoreType.DMA((12, 2)),
            pltpu.SemaphoreType.DMA((12, 2)),
            pltpu.SemaphoreType.DMA((5, 2)),
            pltpu.SemaphoreType.DMA((4,)),
        ],
        compiler_params=pltpu.CompilerParams(
            collective_id=0, has_side_effects=True, vmem_limit_bytes=40 * 1024 * 1024
        ),
        cost_estimate=pl.CostEstimate(flops=1610612736, bytes_accessed=4500000, transcendentals=0),
    )(owner_table, table, grad, left_factor, right_factor, left_root, right_root, live)


def solution(mesh):
    placed = (
        P(None, "fsdp", None),
        P("fsdp", "rep", None),
        P("fsdp", "rep", None),
        P("fsdp", "rep", None),
        P("fsdp", "rep", None),
        P(),
    )
    return jax.shard_map(
        body,
        mesh=mesh,
        in_specs=placed,
        out_specs=(P("fsdp", "rep", None), P("fsdp", "rep", None), P(None, "fsdp", "rep")),
        check_vma=False,
    )
```

time: 198 us -> 103 us (0.52)
  waiting for transfers between devices: 121 us -> 0 us
  Pallas kernels: 0 us -> 89.2 us
  starting transfers between devices: 31.1 us -> 0 us
  matrix products: 15.2 us -> 0 us
  between operations: 14.1 us -> 2.61 us
  other arithmetic: 3.88 us -> 0.2 us
    all_to_all x2 -> x0, waiting for transfers between devices: 120 us -> none  [the longest x1 96.1 us: body(): lax.all_to_all(outgoing, 'fsdp', split_axis=0, concat_axis=1, tiled=True)]
    pallas_call x0 -> x1, Pallas kernels: none -> 89.2 us  [body(): pl.pallas_call(kernel, out_shape=(jax.ShapeDtypeStruct((2, 128, 512), f32...]
    all_to_all x2 -> x0, starting transfers between devices: 31.1 us -> none  [the longest x1 20.6 us: body(): lax.all_to_all(outgoing, 'fsdp', split_axis=0, concat_axis=1, tiled=True)]
    dot_general x4 -> x0, matrix products: 15.2 us -> none  [the longest x1 4.8 us: body(): jnp.einsum('sik,skj->sij', lax.all_gather(left_root, 'rep', axis=1, tiled...]
    unnamed x4 -> x15, local copies, waits for them, and re-layouts: 0.01 us -> 8.33 us
    all_to_all x5 -> x0, local copies, waits for them, and re-layouts: 5.48 us -> none  [the longest x2 3.65 us: body(): lax.all_to_all(outgoing, 'fsdp', split_axis=0, concat_axis=1, tiled=True)]
    gather x2 -> x0, local copies, waits for them, and re-layouts: 3.29 us -> none  [the longest x1 1.85 us: body(): outgoing = jnp.where(filled[:, None, None], grad[source], 0.0)]
    select_n x3 -> x0, other arithmetic: 2.71 us -> none  [the longest x2 2.04 us: body(): outgoing = jnp.where(filled[:, None, None], grad[source], 0.0)]
  transfers between devices with their start and end apart: 3 -> 0, of which waited for: 2 -> 0; matrix products, arithmetic and copies ran while one was open for 6% -> 0% of each run, Pallas kernels for 0% -> 0%
where the time goes in v1:
time: 103 us; the launch traced here: 102 us
  Pallas kernels  89.2 us (87%)
  local copies, waits for them, and re-layouts  9.57 us (9%)
  between operations  2.61 us (3%)
    pallas_call x1, Pallas kernels, body(): pl.pallas_call(kernel, out_shape=(jax.ShapeDtypeStruct((2, 128, 512), f32...  89.2 us
    unnamed x15, local copies, waits for them, and re-layouts  8.33 us

profile of v1, /device:TPU:1, one launch (start us, length us, event | category | flops | bytes accessed | tf_op | source)
XLA Modules:
  0.0 101.6 jit_solution(3362753238499965376)
XLA Ops:
  0.6 0.0 copy-start.5
  0.6 0.6 copy-done.5
  1.3 0.1 select_reduce_fusion.1
  1.4 0.6 dynamic_slice.8
  2.0 0.6 dynamic_slice.7
  4.5 0.1 add_convert_fusion
  4.6 0.1 broadcast_in_dim.34.live_ref
  4.7 0.0 copy-start
  4.7 1.2 %copy-done = f32[128,4,512]{2,1,0:T(4,128)S(1)} copy-done((f32[128,4,512]{2,1,0:T(4,128)S(1)}, f32[128,4,512]{2,1,0:T(4,128)}, u32[]{:S(2)}) %copy-start) | copy-done | bytes 1048600
  5.9 0.0 copy-start.1
  5.9 1.0 %copy-done.1 = f32[2,128,512]{2,1,0:T(8,128)S(1)} copy-done((f32[2,128,512]{2,1,0:T(8,128)S(1)}, f32[2,128,512]{2,1,0:T(8,128)}, u32[]{:S(2)}) %copy-start.1) | copy-done | bytes 524312
  7.0 0.0 copy-start.2
  7.0 1.0 %copy-done.2 = f32[2,128,512]{2,1,0:T(8,128)S(1)} copy-done((f32[2,128,512]{2,1,0:T(8,128)S(1)}, f32[2,128,512]{2,1,0:T(8,128)}, u32[]{:S(2)}) %copy-start.2) | copy-done | bytes 524312
  8.0 0.0 copy-start.3
  8.0 1.0 %copy-done.3 = f32[2,128,512]{2,1,0:T(8,128)S(1)} copy-done((f32[2,128,512]{2,1,0:T(8,128)S(1)}, f32[2,128,512]{2,1,0:T(8,128)}, u32[]{:S(2)}) %copy-start.3) | copy-done | bytes 524312
  9.0 0.0 copy-start.4
  9.0 1.0 %copy-done.4 = f32[2,128,512]{2,1,0:T(8,128)S(1)} copy-done((f32[2,128,512]{2,1,0:T(8,128)S(1)}, f32[2,128,512]{2,1,0:T(8,128)}, u32[]{:S(2)}) %copy-start.4) | copy-done | bytes 524312
  10.1 89.2 %shard_map.85 = (f32[2,128,512]{2,1,0:T(8,128)S(1)}, f32[2,128,512]{2,1,0:T(8,128)S(1)}, f32[128,4,128]{2,1,0:T(4,128)S(1)}) custom-call(s32[128]{0:T(128)S(1)} %copy-done.5, s32[2,128]{1,0:T(2,128)S(1)} %pad_add_fusion.table_ref, f32[128,4,512]{2,1,0:T(4,128)S(1)} %copy-done, f32[2,128,512]{2,1,0:T(8,128)S(1)} %copy-done.1, f32[2,128,512]{2,1,0:T(8,128)S(1)} %copy-done.2, ...), custom_call_target="tpu_custom_call" | custom-call | flops 1610612736 | bytes 4500000 | tf_op jit(solution)/shard_map/pallas_call | solution.py:294
  99.3 0.8 copy.12
  100.1 0.8 copy.13
  100.9 0.7 copy.14
  (2 shorter events, 0.0 us)
Async XLA Ops:
  0.6 0.7 copy-start.5
  4.7 1.2 %copy-start = (f32[128,4,512]{2,1,0:T(4,128)S(1)}, f32[128,4,512]{2,1,0:T(4,128)}, u32[]{:S(2)}) copy-start(f32[128,4,512]{2,1,0:T(4,128)} %grad_ref.1) | copy-start | bytes 3145732
  5.9 1.0 %copy-start.1 = (f32[2,128,512]{2,1,0:T(8,128)S(1)}, f32[2,128,512]{2,1,0:T(8,128)}, u32[]{:S(2)}) copy-start(f32[2,128,512]{2,1,0:T(8,128)} %lf_ref.1) | copy-start | bytes 1572868
  7.0 1.0 %copy-start.2 = (f32[2,128,512]{2,1,0:T(8,128)S(1)}, f32[2,128,512]{2,1,0:T(8,128)}, u32[]{:S(2)}) copy-start(f32[2,128,512]{2,1,0:T(8,128)} %rf_ref.1) | copy-start | bytes 1572868
  8.0 1.0 %copy-start.3 = (f32[2,128,512]{2,1,0:T(8,128)S(1)}, f32[2,128,512]{2,1,0:T(8,128)}, u32[]{:S(2)}) copy-start(f32[2,128,512]{2,1,0:T(8,128)} %lroot_ref.1) | copy-start | bytes 1572868
  9.0 1.0 %copy-start.4 = (f32[2,128,512]{2,1,0:T(8,128)S(1)}, f32[2,128,512]{2,1,0:T(8,128)}, u32[]{:S(2)}) copy-start(f32[2,128,512]{2,1,0:T(8,128)} %rroot_ref.1) | copy-start | bytes 1572868

commit v2 on v0

v2 whole, which is shorter than its diff:
```python
import jax
import jax.numpy as jnp
from jax import lax
from jax.experimental import pallas as pl
from jax.experimental.pallas import tpu as pltpu
from jax.sharding import PartitionSpec as P

moment_decay = 0.9
MESH = pl.DeviceIdType.MESH
bf16 = jnp.bfloat16
f32 = jnp.float32
i32 = jnp.int32

NF, NX = 128, 4
IN, OUT, XA0, XA1, XB0, XB1, XFA, XFB, LA, LB, LFA, LFB = range(12)


def split(x):
    hi = x.astype(bf16)
    return hi, (x - hi.astype(f32)).astype(bf16)


def dot3(a, b, dims):
    def one(p, q):
        return lax.dot_general(p, q, (dims, ((), ())), preferred_element_type=f32)

    return one(a[0], b[0]) + (one(a[0], b[1]) + one(a[1], b[0]))


def kernel(
    owner_ref, row_ref, grad_ref, lf_ref, rf_ref, lroot_ref, rroot_ref,
    left_out, right_out, dir_out,
    gq, send, gbuf, band, ghi, glo, lown, lbuf, lhi, llo, rr, lf, rf, dbuf, rbuf,
    left_new, right_new, dir_new, tab_v, tab_s,
    send_sem, recv_sem, loc_sem, in_sem, out_sem,
):
    me, r = lax.axis_index("fsdp"), lax.axis_index("rep")
    chip, core = lax.div(me, 2), lax.rem(me, 2)
    xa, xb, xc = lax.rem(r + 1, NX), lax.rem(r + 3, NX), lax.rem(r + 2, NX)

    def at128(q):
        return pl.ds(pl.multiple_of(q * 128, 128), 128)

    def load(src, dst, i):
        c = pltpu.make_async_copy(src, dst, in_sem.at[i])
        c.start()
        return c

    in_g = load(grad_ref.at[:, :, at128(r)], gq, 0)
    in_l = load(lroot_ref, lown, 1)
    in_r = load(rroot_ref, rr, 2)
    in_lf = load(lf_ref, lf, 3)
    in_rf = load(rf_ref, rf, 4)

    barrier = pltpu.get_barrier_semaphore()

    @pl.loop(1, NF)
    def _(d):
        pl.semaphore_signal(barrier, inc=1, device_id=(lax.rem(me + d, NF), r), device_id_type=MESH)

    for x in (xa, xb):
        pl.semaphore_signal(barrier, inc=1, device_id=(me, x), device_id_type=MESH)

    owner_of = jnp.transpose(jnp.broadcast_to(row_ref[...], (NF, NF)))
    block = lax.broadcasted_iota(i32, (NF, NF), 0)
    lane = lax.broadcasted_iota(i32, (NF, NF), 1)
    match = owner_of == lane
    first = jnp.min(jnp.where(match, block, NF), axis=0, keepdims=True)
    last = jnp.max(jnp.where(match, block, -1), axis=0, keepdims=True)
    tab_v[0:1, :] = jnp.minimum(first, NF - 1)
    tab_v[1:2, :] = jnp.maximum(last, 0)
    to_s = pltpu.make_async_copy(tab_v, tab_s, loc_sem.at[2, 0])
    to_s.start()
    mine = lane[:1, :] == me
    live0 = jnp.max(jnp.where(mine & (first < NF), 1, 0), axis=1, keepdims=True)
    live1 = jnp.max(jnp.where(mine & (last > first), 1, 0), axis=1, keepdims=True)
    live = (live0, live1)

    def remote(src, dst, kind, k, dev):
        return pltpu.make_async_remote_copy(
            src_ref=src, dst_ref=dst, send_sem=send_sem.at[kind, k], recv_sem=recv_sem.at[kind, k],
            device_id=dev, device_id_type=MESH,
        )

    def wait_bytes(ref, sem):
        pltpu.make_async_copy(ref, ref, sem).wait()

    to_a, to_b = (me, xa), (me, xb)

    to_s.wait()
    in_g.wait()

    def pack(k):
        @pl.loop(0, NF, unroll=8)
        def _(o):
            send[k, o] = gq[tab_s[k, o]]

    pack(0)
    pl.semaphore_wait(barrier, NF - 1 + 2)

    def send_in(k, cc):
        def piece(o):
            remote(send.at[k, o], gbuf.at[k, r, me], IN, k, (o, r)).start()

        @pl.when(core != cc)
        def _():
            piece(chip * 2 + cc)

        @pl.loop(1, NF // 2)
        def _(j):
            piece(lax.rem(chip + j, NF // 2) * 2 + cc)

    def own_copy(src, dst, i, k):
        c = pltpu.make_async_copy(src, dst, loc_sem.at[i, k])
        c.start()
        return c

    own_in = [None, None]
    send_in(0, 0)
    in_l.wait()

    def l_start(k):
        def block_to(q, slot, kind, dev):
            remote(lown.at[k, :, at128(q)], lbuf.at[k, slot], kind, k, dev).start()

        block_to(r, 0, LA, to_b)
        block_to(r, 3, LB, to_a)
        block_to(xa, 1, LA, to_b)
        block_to(xb, 4, LB, to_a)
        if k == 0:
            block_to(xc, 2, LA, to_b)
        else:
            block_to(xc, 2, LB, to_a)

    l_start(0)
    send_in(0, 1)
    own_in[0] = own_copy(send.at[0, me], gbuf.at[0, r, me], 0, 0)
    l_start(1)
    pack(1)
    send_in(1, 0)
    send_in(1, 1)
    own_in[1] = own_copy(send.at[1, me], gbuf.at[1, r, me], 0, 1)

    from_a = (pl.ds(0, 3), pl.ds(0, 2))
    from_b = (pl.ds(3, 2), pl.ds(2, 3))

    def l_forward(k):
        wait_bytes(lbuf.at[k, from_a[k]], recv_sem.at[LA, k])
        remote(lbuf.at[k, 0, pl.ds(0, 64)], lbuf.at[k, 5, pl.ds(0, 64)], LFA, k, to_b).start()
        wait_bytes(lbuf.at[k, from_b[k]], recv_sem.at[LB, k])
        remote(lbuf.at[k, 3, pl.ds(64, 64)], lbuf.at[k, 5, pl.ds(64, 64)], LFB, k, to_a).start()

    def l_put(k, p, q, x):
        hi, lo = split(x)
        lhi[k, at128(p), at128(q)] = hi
        llo[k, at128(p), at128(q)] = lo

    def l_both(k, p, q, x):
        l_put(k, p, q, x)
        l_put(k, q, p, jnp.transpose(x))

    def l_own(k):
        l_put(k, r, r, lown[k, :, at128(r)])
        for q in (xa, xb, xc):
            l_both(k, r, q, lown[k, :, at128(q)])

    def l_take(k):
        l_put(k, xa, xa, lbuf[k, 0])
        l_both(k, xa, xc, lbuf[k, 1])
        if k == 0:
            l_both(k, xa, xb, lbuf[k, 2])
        else:
            l_both(k, xb, xa, lbuf[k, 2])
        l_put(k, xb, xb, lbuf[k, 3])
        l_both(k, xb, xc, lbuf[k, 4])

    def l_end(k):
        wait_bytes(lbuf.at[k, 5, pl.ds(0, 64)], recv_sem.at[LFA, k])
        wait_bytes(lbuf.at[k, 5, pl.ds(64, 64)], recv_sem.at[LFB, k])
        l_put(k, xc, xc, lbuf[k, 5])

    low, high = pl.ds(0, NF // 2), pl.ds(NF // 2, NF // 2)

    def x_start(k):
        wait_bytes(gbuf.at[k, r, pl.ds(0, NF - 1)], recv_sem.at[IN, k])
        own_in[k].wait()
        g0, g1 = gbuf.at[k, r, low], gbuf.at[k, r, high]
        remote(g0, g0, XA0, k, to_a).start()
        remote(g1, g1, XB1, k, to_b).start()
        remote(g1, g1, XA1, k, to_a).start()
        remote(g0, g0, XB0, k, to_b).start()

    def x_forward(k):
        g = gbuf.at[k, xb, low]
        wait_bytes(g, recv_sem.at[XA0, k])
        remote(g, g, XFA, k, to_a).start()
        g = gbuf.at[k, xa, high]
        wait_bytes(g, recv_sem.at[XB1, k])
        remote(g, g, XFB, k, to_b).start()

    def take(k, q):
        @pl.loop(0, 16)
        def _(i):
            for j in range(8):
                band[pl.ds(pl.multiple_of(i * 32, 32) + j * 4, 4), :] = gbuf[k, q, i * 8 + j]

        hi, lo = split(band[...])
        ghi[k, :, at128(q)] = hi
        glo[k, :, at128(q)] = lo

    def x_take(k):
        wait_bytes(gbuf.at[k, xb, high], recv_sem.at[XA1, k])
        take(k, xb)
        wait_bytes(gbuf.at[k, xa, low], recv_sem.at[XB0, k])
        take(k, xa)
        wait_bytes(gbuf.at[k, xc, low], recv_sem.at[XFA, k])
        wait_bytes(gbuf.at[k, xc, high], recv_sem.at[XFB, k])
        take(k, xc)

    def steer(k):
        turned = dot3((ghi[k], glo[k]), split(rr[k]), ((1,), (1,)))
        band[...] = dot3((lhi[k], llo[k]), split(turned), ((1,), (0,)))

        @pl.loop(0, 16)
        def _(i):
            for j in range(8):
                dbuf[k, i * 8 + j] = band[pl.ds(pl.multiple_of(i * 32, 32) + j * 4, 4), :]

    def send_out(k):
        @pl.loop(1, NF)
        def _(d):
            f = lax.rem(me + d, NF)
            remote(dbuf.at[k, f], rbuf.at[k, me], OUT, k, (f, r)).start()

        return own_copy(dbuf.at[k, me], rbuf.at[k, me], 1, k)

    weight = (1.0 - moment_decay) / 512

    def stats(k):
        g = (ghi[k], glo[k])
        term = dot3((ghi[k, at128(r), :], glo[k, at128(r), :]), g, ((1,), (1,)))
        old = lf[k]
        left_new[k] = jnp.where(live[k] > 0, moment_decay * old + weight * term, old)
        term = dot3((ghi[k, :, at128(r)], glo[k, :, at128(r)]), g, ((0,), (0,)))
        old = rf[k]
        right_new[k] = jnp.where(live[k] > 0, moment_decay * old + weight * term, old)

    l_own(0)
    l_own(1)
    l_forward(0)
    l_take(0)
    l_forward(1)
    x_start(0)
    take(0, r)
    x_forward(0)
    l_take(1)
    l_end(0)
    in_r.wait()
    x_take(0)
    steer(0)
    own_out0 = send_out(0)
    l_end(1)
    x_start(1)
    take(1, r)
    x_forward(1)
    x_take(1)
    steer(1)
    own_out1 = send_out(1)
    in_lf.wait()
    in_rf.wait()
    stats(0)
    stats(1)
    out_l = pltpu.make_async_copy(left_new, left_out, out_sem.at[0])
    out_l.start()
    out_r = pltpu.make_async_copy(right_new, right_out, out_sem.at[1])
    out_r.start()

    own_outs = (own_out0, own_out1)
    for k in range(2):
        wait_bytes(rbuf.at[k, pl.ds(0, NF - 1)], recv_sem.at[OUT, k])
        own_outs[k].wait()

    @pl.loop(0, NF, unroll=8)
    def _(b):
        o = owner_ref[b]
        dir_new[b] = rbuf[jnp.where(tab_s[0, o] == b, 0, 1), o]

    out_d = pltpu.make_async_copy(dir_new, dir_out, out_sem.at[2])
    out_d.start()
    for k in range(2):
        wait_bytes(gbuf.at[k, r, pl.ds(0, NF - 1)], send_sem.at[IN, k])
        wait_bytes(rbuf.at[k, pl.ds(0, NF - 1)], send_sem.at[OUT, k])
        for kind in (XA0, XA1, XB0, XB1, XFA, XFB):
            wait_bytes(gbuf.at[k, r, low], send_sem.at[kind, k])
        wait_bytes(lbuf.at[k, from_a[k]], send_sem.at[LA, k])
        wait_bytes(lbuf.at[k, from_b[k]], send_sem.at[LB, k])
        for kind in (LFA, LFB):
            wait_bytes(lbuf.at[k, 5, pl.ds(0, 64)], send_sem.at[kind, k])
    out_l.wait()
    out_r.wait()
    out_d.wait()


def body(grad, left_factor, right_factor, left_root, right_root, owner_table):
    hbm = pl.BlockSpec(memory_space=pltpu.HBM)
    vmem = pl.BlockSpec(memory_space=pltpu.VMEM)
    smem = pl.BlockSpec(memory_space=pltpu.SMEM)
    pieces = (2, NF, 4, 128)
    return pl.pallas_call(
        kernel,
        out_shape=(
            jax.ShapeDtypeStruct((2, 128, 512), f32),
            jax.ShapeDtypeStruct((2, 128, 512), f32),
            jax.ShapeDtypeStruct((NF, 4, 128), f32),
        ),
        in_specs=[smem, vmem] + [hbm] * 5,
        out_specs=(hbm, hbm, hbm),
        scratch_shapes=[
            pltpu.VMEM((NF, 4, 128), f32),
            pltpu.VMEM(pieces, f32),
            pltpu.VMEM((2, NX, NF, 4, 128), f32),
            pltpu.VMEM((512, 128), f32),
            pltpu.VMEM((2, 512, 512), bf16),
            pltpu.VMEM((2, 512, 512), bf16),
            pltpu.VMEM((2, 128, 512), f32),
            pltpu.VMEM((2, 6, 128, 128), f32),
            pltpu.VMEM((2, 512, 512), bf16),
            pltpu.VMEM((2, 512, 512), bf16),
            pltpu.VMEM((2, 128, 512), f32),
            pltpu.VMEM((2, 128, 512), f32),
            pltpu.VMEM((2, 128, 512), f32),
            pltpu.VMEM(pieces, f32),
            pltpu.VMEM(pieces, f32),
            pltpu.VMEM((2, 128, 512), f32),
            pltpu.VMEM((2, 128, 512), f32),
            pltpu.VMEM((NF, 4, 128), f32),
            pltpu.VMEM((8, 128), i32),
            pltpu.SMEM((8, 128), i32),
            pltpu.SemaphoreType.DMA((12, 2)),
            pltpu.SemaphoreType.DMA((12, 2)),
            pltpu.SemaphoreType.DMA((3, 2)),
            pltpu.SemaphoreType.DMA((5,)),
            pltpu.SemaphoreType.DMA((3,)),
        ],
        compiler_params=pltpu.CompilerParams(
            collective_id=0, has_side_effects=True, vmem_limit_bytes=56 * 1024 * 1024
        ),
        cost_estimate=pl.CostEstimate(flops=1610612736, bytes_accessed=4500000, transcendentals=0),
    )(owner_table, owner_table.reshape(1, NF), grad, left_factor, right_factor, left_root, right_root)


def solution(mesh):
    placed = (
        P(None, "fsdp", None),
        P("fsdp", "rep", None),
        P("fsdp", "rep", None),
        P("fsdp", "rep", None),
        P("fsdp", "rep", None),
        P(),
    )
    return jax.shard_map(
        body,
        mesh=mesh,
        in_specs=placed,
        out_specs=(P("fsdp", "rep", None), P("fsdp", "rep", None), P(None, "fsdp", "rep")),
        check_vma=False,
    )
```

time: 198 us -> 84.5 us (0.43)
  waiting for transfers between devices: 121 us -> 0 us
  Pallas kernels: 0 us -> 80 us
  starting transfers between devices: 31.1 us -> 0 us
  matrix products: 15.2 us -> 0 us
  between operations: 14.1 us -> 0.65 us
  local copies, waits for them, and re-layouts: 10.9 us -> 3.72 us
  other arithmetic: 3.88 us -> 0 us
    all_to_all x2 -> x0, waiting for transfers between devices: 120 us -> none  [the longest x1 96.1 us: body(): lax.all_to_all(outgoing, 'fsdp', split_axis=0, concat_axis=1, tiled=True)]
    pallas_call x0 -> x1, Pallas kernels: none -> 80 us  [body(): pl.pallas_call(kernel, out_shape=(jax.ShapeDtypeStruct((2, 128, 512), f32...]
    all_to_all x2 -> x0, starting transfers between devices: 31.1 us -> none  [the longest x1 20.6 us: body(): lax.all_to_all(outgoing, 'fsdp', split_axis=0, concat_axis=1, tiled=True)]
    dot_general x4 -> x0, matrix products: 15.2 us -> none  [the longest x1 4.8 us: body(): jnp.einsum('sik,skj->sij', lax.all_gather(left_root, 'rep', axis=1, tiled...]
    all_to_all x5 -> x0, local copies, waits for them, and re-layouts: 5.48 us -> none  [the longest x2 3.65 us: body(): lax.all_to_all(outgoing, 'fsdp', split_axis=0, concat_axis=1, tiled=True)]
    unnamed x4 -> x7, local copies, waits for them, and re-layouts: 0.01 us -> 3.72 us
    gather x2 -> x0, local copies, waits for them, and re-layouts: 3.29 us -> none  [the longest x1 1.85 us: body(): outgoing = jnp.where(filled[:, None, None], grad[source], 0.0)]
    select_n x3 -> x0, other arithmetic: 2.71 us -> none  [the longest x2 2.04 us: body(): outgoing = jnp.where(filled[:, None, None], grad[source], 0.0)]
  transfers between devices with their start and end apart: 3 -> 0, of which waited for: 2 -> 0; matrix products, arithmetic and copies ran while one was open for 6% -> 0% of each run, Pallas kernels for 0% -> 0%
where the time goes in v2:
time: 84.5 us; the launch traced here: 84.4 us
  Pallas kernels  80 us (95%)
  local copies, waits for them, and re-layouts  3.72 us (4%)
    pallas_call x1, Pallas kernels, body(): pl.pallas_call(kernel, out_shape=(jax.ShapeDtypeStruct((2, 128, 512), f32...  80 us
    unnamed x7, local copies, waits for them, and re-layouts  3.72 us

profile of v2, /device:TPU:1, one launch (start us, length us, event | category | flops | bytes accessed | tf_op | source)
XLA Modules:
  0.0 84.4 jit_solution(1431917881760394556)
XLA Ops:
  0.6 80.0 %shard_map.85 = (f32[2,128,512]{2,1,0:T(8,128)}, f32[2,128,512]{2,1,0:T(8,128)}, f32[128,4,128]{2,1,0:T(4,128)}) custom-call(s32[128]{0:T(128)} %owner_ref.1, s32[1,128]{1,0:T(1,128)} %bitcast.1, f32[128,4,512]{2,1,0:T(4,128)} %grad_ref.1, f32[2,128,512]{2,1,0:T(8,128)} %lf_ref.1, f32[2,128,512]{2,1,0:T(8,128)} %rf_ref.1, f32[2,128,512]{2,1,0:T(8,128)} %lroot_ref.1, ...), custom_call_target="tpu_custom_call" | custom-call | flops 1610612736 | bytes 4500000 | tf_op jit(solution)/shard_map/pallas_call | solution.py:309
  80.6 0.0 copy-start
  80.6 1.9 %copy.12 = f32[2,128,512]{2,1,0:T(8,128)} copy(f32[2,128,512]{2,1,0:T(8,128)} %get-tuple-element.6) | data formatting | bytes 1048576
  82.6 0.0 copy-done
  82.6 0.0 copy-start.1
  82.6 0.8 copy.13
  83.4 0.3 copy-done.1
  83.7 0.7 copy.14
Async XLA Ops:
  80.6 1.9 %copy-start = (f32[2,128,512]{2,1,0:T(8,128)S(1)}, f32[2,128,512]{2,1,0:T(8,128)}, u32[]{:S(2)}) copy-start(f32[2,128,512]{2,1,0:T(8,128)} %get-tuple-element.7) | copy-start | bytes 1572868
  82.6 1.1 %copy-start.1 = (f32[128,4,128]{2,1,0:T(4,128)S(1)}, f32[128,4,128]{2,1,0:T(4,128)}, u32[]{:S(2)}) copy-start(f32[128,4,128]{2,1,0:T(4,128)} %get-tuple-element.8) | copy-start | bytes 786436

commit v3 on v2

--- a/solution.py
+++ b/solution.py
@@ -12,7 +12,8 @@
 i32 = jnp.int32
 
 NF, NX = 128, 4
-IN, OUT, XA0, XA1, XB0, XB1, XFA, XFB, LA, LB, LFA, LFB = range(12)
+IN0, IN1, OUT, LA, LB, LFA, LFB = range(7)
+XA0, XA1, XB0, XB1, XFA, XFB = range(6)
 
 
 def split(x):
@@ -30,9 +31,9 @@
 def kernel(
     owner_ref, row_ref, grad_ref, lf_ref, rf_ref, lroot_ref, rroot_ref,
     left_out, right_out, dir_out,
-    gq, send, gbuf, band, ghi, glo, lown, lbuf, lhi, llo, rr, lf, rf, dbuf, rbuf,
+    gq, send, gbuf, band, acc, ghi, glo, lown, lbuf, lhi, llo, rr, rhi, rlo, lf, rf, dbuf, rbuf,
     left_new, right_new, dir_new, tab_v, tab_s,
-    send_sem, recv_sem, loc_sem, in_sem, out_sem,
+    send_sem, recv_sem, x_send_sem, x_recv_sem, loc_sem, in_sem, out_sem,
 ):
     me, r = lax.axis_index("fsdp"), lax.axis_index("rep")
     chip, core = lax.div(me, 2), lax.rem(me, 2)
@@ -54,9 +55,15 @@
 
     barrier = pltpu.get_barrier_semaphore()
 
-    @pl.loop(1, NF)
-    def _(d):
-        pl.semaphore_signal(barrier, inc=1, device_id=(lax.rem(me + d, NF), r), device_id_type=MESH)
+    @pl.loop(0, NF // 8)
+    def _(t):
+        far = NF // 16 + lax.div(t + 1, 2) * (1 - 2 * lax.rem(t, 2))
+        for i in range(8):
+            f = lax.rem(me + far * 8 + i, NF)
+
+            @pl.when(f != me)
+            def _():
+                pl.semaphore_signal(barrier, inc=1, device_id=(f, r), device_id_type=MESH)
 
     for x in (xa, xb):
         pl.semaphore_signal(barrier, inc=1, device_id=(me, x), device_id_type=MESH)
@@ -99,16 +106,22 @@
     pl.semaphore_wait(barrier, NF - 1 + 2)
 
     def send_in(k, cc):
-        def piece(o):
-            remote(send.at[k, o], gbuf.at[k, r, me], IN, k, (o, r)).start()
-
         @pl.when(core != cc)
         def _():
-            piece(chip * 2 + cc)
-
-        @pl.loop(1, NF // 2)
+            o = chip * 2 + cc
+            remote(send.at[k, o], gbuf.at[k, r, core], IN1, k, (o, r)).start()
+
+        def piece(j, kind):
+            o = lax.rem(chip + j, NF // 2) * 2 + cc
+            remote(send.at[k, o], gbuf.at[k, r, (NF // 2 - j) * 2 + core], kind, k, (o, r)).start()
+
+        @pl.loop(1, 33)
         def _(j):
-            piece(lax.rem(chip + j, NF // 2) * 2 + cc)
+            piece(j, IN0)
+
+        @pl.loop(33, NF // 2)
+        def _(j):
+            piece(j, IN1)
 
     def own_copy(src, dst, i, k):
         c = pltpu.make_async_copy(src, dst, loc_sem.at[i, k])
@@ -134,12 +147,12 @@
 
     l_start(0)
     send_in(0, 1)
-    own_in[0] = own_copy(send.at[0, me], gbuf.at[0, r, me], 0, 0)
+    own_in[0] = own_copy(send.at[0, me], gbuf.at[0, r, core], 0, 0)
     l_start(1)
     pack(1)
     send_in(1, 0)
     send_in(1, 1)
-    own_in[1] = own_copy(send.at[1, me], gbuf.at[1, r, me], 0, 1)
+    own_in[1] = own_copy(send.at[1, me], gbuf.at[1, r, core], 0, 1)
 
     from_a = (pl.ds(0, 3), pl.ds(0, 2))
     from_b = (pl.ds(3, 2), pl.ds(2, 3))
@@ -179,58 +192,86 @@
         wait_bytes(lbuf.at[k, 5, pl.ds(64, 64)], recv_sem.at[LFB, k])
         l_put(k, xc, xc, lbuf[k, 5])
 
-    low, high = pl.ds(0, NF // 2), pl.ds(NF // 2, NF // 2)
-
-    def x_start(k):
-        wait_bytes(gbuf.at[k, r, pl.ds(0, NF - 1)], recv_sem.at[IN, k])
-        own_in[k].wait()
-        g0, g1 = gbuf.at[k, r, low], gbuf.at[k, r, high]
-        remote(g0, g0, XA0, k, to_a).start()
-        remote(g1, g1, XB1, k, to_b).start()
-        remote(g1, g1, XA1, k, to_a).start()
-        remote(g0, g0, XB0, k, to_b).start()
-
-    def x_forward(k):
-        g = gbuf.at[k, xb, low]
-        wait_bytes(g, recv_sem.at[XA0, k])
-        remote(g, g, XFA, k, to_a).start()
-        g = gbuf.at[k, xa, high]
-        wait_bytes(g, recv_sem.at[XB1, k])
-        remote(g, g, XFB, k, to_b).start()
-
-    def take(k, q):
-        @pl.loop(0, 16)
+    half_at = (64, 0)
+
+    def quarters(k, q, h):
+        return gbuf.at[k, q, pl.ds(half_at[h], 32)], gbuf.at[k, q, pl.ds(half_at[h] + 32, 32)]
+
+    def x_remote(ref, kind, k, h, dev):
+        pltpu.make_async_remote_copy(
+            src_ref=ref, dst_ref=ref, send_sem=x_send_sem.at[kind, k, h], recv_sem=x_recv_sem.at[kind, k, h],
+            device_id=dev, device_id_type=MESH,
+        ).start()
+
+    def x_start(k, h):
+        if h == 0:
+            wait_bytes(gbuf.at[k, r, pl.ds(64, 64)], recv_sem.at[IN0, k])
+        else:
+            wait_bytes(gbuf.at[k, r, pl.ds(0, 63)], recv_sem.at[IN1, k])
+            own_in[k].wait()
+        g0, g1 = quarters(k, r, h)
+        x_remote(g0, XA0, k, h, to_a)
+        x_remote(g1, XB1, k, h, to_b)
+        x_remote(g1, XA1, k, h, to_a)
+        x_remote(g0, XB0, k, h, to_b)
+
+    def x_forward(k, h):
+        g0, _ = quarters(k, xb, h)
+        wait_bytes(g0, x_recv_sem.at[XA0, k, h])
+        x_remote(g0, XFA, k, h, to_a)
+        _, g1 = quarters(k, xa, h)
+        wait_bytes(g1, x_recv_sem.at[XB1, k, h])
+        x_remote(g1, XFB, k, h, to_b)
+
+    def take(k, q, start=False):
+        @pl.loop(0, 8)
         def _(i):
             for j in range(8):
-                band[pl.ds(pl.multiple_of(i * 32, 32) + j * 4, 4), :] = gbuf[k, q, i * 8 + j]
-
-        hi, lo = split(band[...])
-        ghi[k, :, at128(q)] = hi
-        glo[k, :, at128(q)] = lo
+                m = i * 8 + j
+                base = pl.multiple_of(lax.rem(chip + m, NF // 2) * 8, 8)
+                band[pl.ds(base, 4), :] = gbuf[k, q, 2 * m]
+                band[pl.ds(base + 4, 4), :] = gbuf[k, q, 2 * m + 1]
+
+        g = split(band[...])
+        ghi[k, :, at128(q)], glo[k, :, at128(q)] = g
+        part = dot3(g, (rhi[k, at128(q), :], rlo[k, at128(q), :]), ((1,), (0,)))
+        if start:
+            acc[...] = part
+        else:
+            acc[...] += part
 
     def x_take(k):
-        wait_bytes(gbuf.at[k, xb, high], recv_sem.at[XA1, k])
+        for h in range(2):
+            _, g1 = quarters(k, xb, h)
+            wait_bytes(g1, x_recv_sem.at[XA1, k, h])
         take(k, xb)
-        wait_bytes(gbuf.at[k, xa, low], recv_sem.at[XB0, k])
+        for h in range(2):
+            g0, _ = quarters(k, xa, h)
+            wait_bytes(g0, x_recv_sem.at[XB0, k, h])
         take(k, xa)
-        wait_bytes(gbuf.at[k, xc, low], recv_sem.at[XFA, k])
-        wait_bytes(gbuf.at[k, xc, high], recv_sem.at[XFB, k])
+        for h in range(2):
+            g0, g1 = quarters(k, xc, h)
+            wait_bytes(g0, x_recv_sem.at[XFA, k, h])
+            wait_bytes(g1, x_recv_sem.at[XFB, k, h])
         take(k, xc)
 
-    def steer(k):
-        turned = dot3((ghi[k], glo[k]), split(rr[k]), ((1,), (1,)))
-        band[...] = dot3((lhi[k], llo[k]), split(turned), ((1,), (0,)))
-
-        @pl.loop(0, 16)
+    def steer_and_send(k):
+        t = split(acc[...])
+
+        @pl.loop(0, 4)
         def _(i):
-            for j in range(8):
-                dbuf[k, i * 8 + j] = band[pl.ds(pl.multiple_of(i * 32, 32) + j * 4, 4), :]
-
-    def send_out(k):
-        @pl.loop(1, NF)
-        def _(d):
-            f = lax.rem(me + d, NF)
-            remote(dbuf.at[k, f], rbuf.at[k, me], OUT, k, (f, r)).start()
+            p = lax.rem(lax.div(chip, 16) + i, 4)
+            band[pl.ds(0, 128), :] = dot3((lhi[k, at128(p), :], llo[k, at128(p), :]), t, ((1,), (0,)))
+            for j in range(32):
+                dbuf[k, p * 32 + j] = band[pl.ds(j * 4, 4), :]
+
+            @pl.loop(0, 32)
+            def _(j):
+                f = p * 32 + lax.rem(me + j, 32)
+
+                @pl.when(f != me)
+                def _():
+                    remote(dbuf.at[k, f], rbuf.at[k, me], OUT, k, (f, r)).start()
 
         return own_copy(dbuf.at[k, me], rbuf.at[k, me], 1, k)
 
@@ -247,25 +288,29 @@
 
     l_own(0)
     l_own(1)
+    in_r.wait()
+    for k in range(2):
+        rhi[k], rlo[k] = split(jnp.transpose(rr[k]))
     l_forward(0)
     l_take(0)
+    x_start(0, 0)
+    x_start(0, 1)
+    take(0, r, True)
+    x_forward(0, 0)
     l_forward(1)
-    x_start(0)
-    take(0, r)
-    x_forward(0)
+    x_forward(0, 1)
+    l_end(0)
+    x_take(0)
+    own_out0 = steer_and_send(0)
     l_take(1)
-    l_end(0)
-    in_r.wait()
-    x_take(0)
-    steer(0)
-    own_out0 = send_out(0)
     l_end(1)
-    x_start(1)
-    take(1, r)
-    x_forward(1)
+    x_start(1, 0)
+    x_start(1, 1)
+    take(1, r, True)
+    x_forward(1, 0)
+    x_forward(1, 1)
     x_take(1)
-    steer(1)
-    own_out1 = send_out(1)
+    own_out1 = steer_and_send(1)
     in_lf.wait()
     in_rf.wait()
     stats(0)
@@ -288,10 +333,12 @@
     out_d = pltpu.make_async_copy(dir_new, dir_out, out_sem.at[2])
     out_d.start()
     for k in range(2):
-        wait_bytes(gbuf.at[k, r, pl.ds(0, NF - 1)], send_sem.at[IN, k])
+        wait_bytes(gbuf.at[k, r, pl.ds(64, 64)], send_sem.at[IN0, k])
+        wait_bytes(gbuf.at[k, r, pl.ds(0, 63)], send_sem.at[IN1, k])
         wait_bytes(rbuf.at[k, pl.ds(0, NF - 1)], send_sem.at[OUT, k])
         for kind in (XA0, XA1, XB0, XB1, XFA, XFB):
-            wait_bytes(gbuf.at[k, r, low], send_sem.at[kind, k])
+            for h in range(2):
+                wait_bytes(gbuf.at[k, r, pl.ds(0, 32)], x_send_sem.at[kind, k, h])
         wait_bytes(lbuf.at[k, from_a[k]], send_sem.at[LA, k])
         wait_bytes(lbuf.at[k, from_b[k]], send_sem.at[LB, k])
         for kind in (LFA, LFB):
@@ -301,12 +348,23 @@
     out_d.wait()
 
 
+def copy_out(a, b, c, a_out, b_out, c_out, sem):
+    copies = [
+        pltpu.make_async_copy(src, dst, sem.at[i])
+        for i, (src, dst) in enumerate(((a, a_out), (b, b_out), (c, c_out)))
+    ]
+    for c in copies:
+        c.start()
+    for c in copies:
+        c.wait()
+
+
 def body(grad, left_factor, right_factor, left_root, right_root, owner_table):
     hbm = pl.BlockSpec(memory_space=pltpu.HBM)
     vmem = pl.BlockSpec(memory_space=pltpu.VMEM)
     smem = pl.BlockSpec(memory_space=pltpu.SMEM)
     pieces = (2, NF, 4, 128)
-    return pl.pallas_call(
+    results = pl.pallas_call(
         kernel,
         out_shape=(
             jax.ShapeDtypeStruct((2, 128, 512), f32),
@@ -320,6 +378,7 @@
             pltpu.VMEM(pieces, f32),
             pltpu.VMEM((2, NX, NF, 4, 128), f32),
             pltpu.VMEM((512, 128), f32),
+            pltpu.VMEM((512, 128), f32),
             pltpu.VMEM((2, 512, 512), bf16),
             pltpu.VMEM((2, 512, 512), bf16),
             pltpu.VMEM((2, 128, 512), f32),
@@ -327,6 +386,8 @@
             pltpu.VMEM((2, 512, 512), bf16),
             pltpu.VMEM((2, 512, 512), bf16),
             pltpu.VMEM((2, 128, 512), f32),
+            pltpu.VMEM((2, 512, 128), bf16),
+            pltpu.VMEM((2, 512, 128), bf16),
             pltpu.VMEM((2, 128, 512), f32),
             pltpu.VMEM((2, 128, 512), f32),
             pltpu.VMEM(pieces, f32),
@@ -336,8 +397,10 @@
             pltpu.VMEM((NF, 4, 128), f32),
             pltpu.VMEM((8, 128), i32),
             pltpu.SMEM((8, 128), i32),
-            pltpu.SemaphoreType.DMA((12, 2)),
-            pltpu.SemaphoreType.DMA((12, 2)),
+            pltpu.SemaphoreType.DMA((7, 2)),
+            pltpu.SemaphoreType.DMA((7, 2)),
+            pltpu.SemaphoreType.DMA((6, 2, 2)),
+            pltpu.SemaphoreType.DMA((6, 2, 2)),
             pltpu.SemaphoreType.DMA((3, 2)),
             pltpu.SemaphoreType.DMA((5,)),
             pltpu.SemaphoreType.DMA((3,)),
@@ -347,6 +410,15 @@
         ),
         cost_estimate=pl.CostEstimate(flops=1610612736, bytes_accessed=4500000, transcendentals=0),
     )(owner_table, owner_table.reshape(1, NF), grad, left_factor, right_factor, left_root, right_root)
+    shapes = tuple(jax.ShapeDtypeStruct(x.shape, x.dtype) for x in results)
+    return pl.pallas_call(
+        copy_out,
+        out_shape=shapes,
+        in_specs=[hbm] * 3,
+        out_specs=(hbm,) * 3,
+        scratch_shapes=[pltpu.SemaphoreType.DMA((3,))],
+        compiler_params=pltpu.CompilerParams(vmem_limit_bytes=56 * 1024 * 1024),
+    )(*results)
 
 
 def solution(mesh):

time: 84.5 us -> 118 us (1.40)
  Pallas kernels: 80 us -> 118 us
  local copies, waits for them, and re-layouts: 3.72 us -> 0 us
    pallas_call x0 -> x1, Pallas kernels: none -> 40.8 us  [body(): pl.pallas_call(copy_out, out_shape=shapes, in_specs=[hbm] * 3, out_specs=...]
    unnamed x7 -> x0, local copies, waits for them, and re-layouts: 3.72 us -> none
    pallas_call x1, Pallas kernels: 80 us -> 76.7 us  [body(): pl.pallas_call(kernel, out_shape=(jax.ShapeDtypeStruct((2, 128, 512), f32...]
where the time goes in v3:
time: 118 us
  Pallas kernels  118 us (100%)
    pallas_call x1, Pallas kernels, body(): pl.pallas_call(kernel, out_shape=(jax.ShapeDtypeStruct((2, 128, 512), f32...  76.7 us
    pallas_call x1, Pallas kernels, body(): pl.pallas_call(copy_out, out_shape=shapes, in_specs=[hbm] * 3, out_specs=...  40.8 us

profile of v3, /device:TPU:1, one launch (start us, length us, event | category | flops | bytes accessed | tf_op | source)
XLA Modules:
  0.0 118.2 jit_solution(4454651726208711501)
XLA Ops:
  0.6 76.7 %shard_map.85 = (f32[2,128,512]{2,1,0:T(8,128)}, f32[2,128,512]{2,1,0:T(8,128)}, f32[128,4,128]{2,1,0:T(4,128)}) custom-call(s32[128]{0:T(128)} %owner_ref.1, s32[1,128]{1,0:T(1,128)} %bitcast.1, f32[128,4,512]{2,1,0:T(4,128)} %grad_ref.1, f32[2,128,512]{2,1,0:T(8,128)} %lf_ref.1, f32[2,128,512]{2,1,0:T(8,128)} %rf_ref.1, f32[2,128,512]{2,1,0:T(8,128)} %lroot_ref.1, ...), custom_call_target="tpu_custom_call" | custom-call | flops 1610612736 | bytes 4500000 | tf_op jit(solution)/shard_map/pallas_call | solution.py:367
  77.4 40.8 %shard_map.86 = (f32[2,128,512]{2,1,0:T(8,128)}, f32[2,128,512]{2,1,0:T(8,128)}, f32[128,4,128]{2,1,0:T(4,128)}) custom-call(f32[2,128,512]{2,1,0:T(8,128)} %get-tuple-element.6.a, f32[2,128,512]{2,1,0:T(8,128)} %get-tuple-element.7.b, f32[128,4,128]{2,1,0:T(4,128)} %get-tuple-element.8.c), custom_call_target="tpu_custom_call" | custom-call | tf_op jit(solution)/shard_map/pallas_call | solution.py:414

commit v4 on v3

--- a/solution.py
+++ b/solution.py
@@ -29,10 +29,10 @@
 
 
 def kernel(
-    owner_ref, row_ref, grad_ref, lf_ref, rf_ref, lroot_ref, rroot_ref,
+    row_ref, grad_ref, lf_ref, rf_ref, lroot_ref, rroot_ref,
     left_out, right_out, dir_out,
     gq, send, gbuf, band, acc, ghi, glo, lown, lbuf, lhi, llo, rr, rhi, rlo, lf, rf, dbuf, rbuf,
-    left_new, right_new, dir_new, tab_v, tab_s,
+    left_new, right_new, dir_new, row_v, tab_v, tab_s,
     send_sem, recv_sem, x_send_sem, x_recv_sem, loc_sem, in_sem, out_sem,
 ):
     me, r = lax.axis_index("fsdp"), lax.axis_index("rep")
@@ -47,6 +47,7 @@
         c.start()
         return c
 
+    in_o = load(row_ref, row_v, 5)
     in_g = load(grad_ref.at[:, :, at128(r)], gq, 0)
     in_l = load(lroot_ref, lown, 1)
     in_r = load(rroot_ref, rr, 2)
@@ -68,7 +69,9 @@
     for x in (xa, xb):
         pl.semaphore_signal(barrier, inc=1, device_id=(me, x), device_id_type=MESH)
 
-    owner_of = jnp.transpose(jnp.broadcast_to(row_ref[...], (NF, NF)))
+    in_o.wait()
+    row = row_v[...]
+    owner_of = jnp.transpose(jnp.broadcast_to(row, (NF, NF)))
     block = lax.broadcasted_iota(i32, (NF, NF), 0)
     lane = lax.broadcasted_iota(i32, (NF, NF), 1)
     match = owner_of == lane
@@ -76,6 +79,8 @@
     last = jnp.max(jnp.where(match, block, -1), axis=0, keepdims=True)
     tab_v[0:1, :] = jnp.minimum(first, NF - 1)
     tab_v[1:2, :] = jnp.maximum(last, 0)
+    later = jnp.max(jnp.where((owner_of == row) & (block < lane), 1, 0), axis=0, keepdims=True)
+    tab_v[2:3, :] = later * NF + row
     to_s = pltpu.make_async_copy(tab_v, tab_s, loc_sem.at[2, 0])
     to_s.start()
     mine = lane[:1, :] == me
@@ -115,7 +120,7 @@
             o = lax.rem(chip + j, NF // 2) * 2 + cc
             remote(send.at[k, o], gbuf.at[k, r, (NF // 2 - j) * 2 + core], kind, k, (o, r)).start()
 
-        @pl.loop(1, 33)
+        @pl.loop(1, 33, unroll=4)
         def _(j):
             piece(j, IN0)
 
@@ -240,7 +245,7 @@
         else:
             acc[...] += part
 
-    def x_take(k):
+    def x_take_near(k):
         for h in range(2):
             _, g1 = quarters(k, xb, h)
             wait_bytes(g1, x_recv_sem.at[XA1, k, h])
@@ -249,6 +254,8 @@
             g0, _ = quarters(k, xa, h)
             wait_bytes(g0, x_recv_sem.at[XB0, k, h])
         take(k, xa)
+
+    def x_take_far(k):
         for h in range(2):
             g0, g1 = quarters(k, xc, h)
             wait_bytes(g0, x_recv_sem.at[XFA, k, h])
@@ -265,15 +272,17 @@
             for j in range(32):
                 dbuf[k, p * 32 + j] = band[pl.ds(j * 4, 4), :]
 
-            @pl.loop(0, 32)
-            def _(j):
+            def piece(j):
                 f = p * 32 + lax.rem(me + j, 32)
-
-                @pl.when(f != me)
-                def _():
-                    remote(dbuf.at[k, f], rbuf.at[k, me], OUT, k, (f, r)).start()
-
-        return own_copy(dbuf.at[k, me], rbuf.at[k, me], 1, k)
+                remote(dbuf.at[k, f], rbuf.at[k * NF + me], OUT, k, (f, r)).start()
+
+            @pl.when(i > 0)
+            def _():
+                piece(0)
+
+            pl.loop(1, 32)(piece)
+
+        return own_copy(dbuf.at[k, me], rbuf.at[k * NF + me], 1, k)
 
     weight = (1.0 - moment_decay) / 512
 
@@ -300,16 +309,18 @@
     l_forward(1)
     x_forward(0, 1)
     l_end(0)
-    x_take(0)
+    x_take_near(0)
+    x_start(1, 0)
+    x_take_far(0)
     own_out0 = steer_and_send(0)
+    x_start(1, 1)
+    x_forward(1, 0)
+    take(1, r, True)
+    x_forward(1, 1)
     l_take(1)
     l_end(1)
-    x_start(1, 0)
-    x_start(1, 1)
-    take(1, r, True)
-    x_forward(1, 0)
-    x_forward(1, 1)
-    x_take(1)
+    x_take_near(1)
+    x_take_far(1)
     own_out1 = steer_and_send(1)
     in_lf.wait()
     in_rf.wait()
@@ -322,20 +333,19 @@
 
     own_outs = (own_out0, own_out1)
     for k in range(2):
-        wait_bytes(rbuf.at[k, pl.ds(0, NF - 1)], recv_sem.at[OUT, k])
+        wait_bytes(rbuf.at[pl.ds(k * NF, NF - 1)], recv_sem.at[OUT, k])
         own_outs[k].wait()
 
     @pl.loop(0, NF, unroll=8)
     def _(b):
-        o = owner_ref[b]
-        dir_new[b] = rbuf[jnp.where(tab_s[0, o] == b, 0, 1), o]
+        dir_new[b] = rbuf[tab_s[2, b]]
 
     out_d = pltpu.make_async_copy(dir_new, dir_out, out_sem.at[2])
     out_d.start()
     for k in range(2):
         wait_bytes(gbuf.at[k, r, pl.ds(64, 64)], send_sem.at[IN0, k])
         wait_bytes(gbuf.at[k, r, pl.ds(0, 63)], send_sem.at[IN1, k])
-        wait_bytes(rbuf.at[k, pl.ds(0, NF - 1)], send_sem.at[OUT, k])
+        wait_bytes(rbuf.at[pl.ds(k * NF, NF - 1)], send_sem.at[OUT, k])
         for kind in (XA0, XA1, XB0, XB1, XFA, XFB):
             for h in range(2):
                 wait_bytes(gbuf.at[k, r, pl.ds(0, 32)], x_send_sem.at[kind, k, h])
@@ -361,8 +371,6 @@
 
 def body(grad, left_factor, right_factor, left_root, right_root, owner_table):
     hbm = pl.BlockSpec(memory_space=pltpu.HBM)
-    vmem = pl.BlockSpec(memory_space=pltpu.VMEM)
-    smem = pl.BlockSpec(memory_space=pltpu.SMEM)
     pieces = (2, NF, 4, 128)
     results = pl.pallas_call(
         kernel,
@@ -371,7 +379,7 @@
             jax.ShapeDtypeStruct((2, 128, 512), f32),
             jax.ShapeDtypeStruct((NF, 4, 128), f32),
         ),
-        in_specs=[smem, vmem] + [hbm] * 5,
+        in_specs=[hbm] * 6,
         out_specs=(hbm, hbm, hbm),
         scratch_shapes=[
             pltpu.VMEM((NF, 4, 128), f32),
@@ -391,10 +399,11 @@
             pltpu.VMEM((2, 128, 512), f32),
             pltpu.VMEM((2, 128, 512), f32),
             pltpu.VMEM(pieces, f32),
-            pltpu.VMEM(pieces, f32),
+            pltpu.VMEM((2 * NF, 4, 128), f32),
             pltpu.VMEM((2, 128, 512), f32),
             pltpu.VMEM((2, 128, 512), f32),
             pltpu.VMEM((NF, 4, 128), f32),
+            pltpu.VMEM((1, 128), i32),
             pltpu.VMEM((8, 128), i32),
             pltpu.SMEM((8, 128), i32),
             pltpu.SemaphoreType.DMA((7, 2)),
@@ -402,14 +411,14 @@
             pltpu.SemaphoreType.DMA((6, 2, 2)),
             pltpu.SemaphoreType.DMA((6, 2, 2)),
             pltpu.SemaphoreType.DMA((3, 2)),
-            pltpu.SemaphoreType.DMA((5,)),
+            pltpu.SemaphoreType.DMA((6,)),
             pltpu.SemaphoreType.DMA((3,)),
         ],
         compiler_params=pltpu.CompilerParams(
-            collective_id=0, has_side_effects=True, vmem_limit_bytes=56 * 1024 * 1024
+            collective_id=0, has_side_effects=True, vmem_limit_bytes=55050240
         ),
         cost_estimate=pl.CostEstimate(flops=1610612736, bytes_accessed=4500000, transcendentals=0),
-    )(owner_table, owner_table.reshape(1, NF), grad, left_factor, right_factor, left_root, right_root)
+    )(owner_table.reshape(1, NF), grad, left_factor, right_factor, left_root, right_root)
     shapes = tuple(jax.ShapeDtypeStruct(x.shape, x.dtype) for x in results)
     return pl.pallas_call(
         copy_out,
@@ -417,7 +426,7 @@
         in_specs=[hbm] * 3,
         out_specs=(hbm,) * 3,
         scratch_shapes=[pltpu.SemaphoreType.DMA((3,))],
-        compiler_params=pltpu.CompilerParams(vmem_limit_bytes=56 * 1024 * 1024),
+        compiler_params=pltpu.CompilerParams(vmem_limit_bytes=4 * 1024 * 1024),
     )(*results)
 
 

time: 118 us -> 78.3 us (0.66)
  Pallas kernels: 118 us -> 76.9 us
    pallas_call x1, Pallas kernels: 40.8 us -> 1.08 us  [body(): pl.pallas_call(copy_out, out_shape=shapes, in_specs=[hbm] * 3, out_specs=...]
where the time goes in v4:
time: 78.3 us; the launch traced here: 78.2 us
  Pallas kernels  76.9 us (98%)
    pallas_call x1, Pallas kernels, body(): pl.pallas_call(kernel, out_shape=(jax.ShapeDtypeStruct((2, 128, 512), f32...  75.8 us

profile of v4, /device:TPU:1, one launch (start us, length us, event | category | flops | bytes accessed | tf_op | source)
XLA Modules:
  0.0 78.2 jit_solution(895816845334312101)
XLA Ops:
  0.6 0.0 copy-start
  0.6 0.6 copy-done
  1.3 75.8 %shard_map.85 = (f32[2,128,512]{2,1,0:T(8,128)S(1)}, f32[2,128,512]{2,1,0:T(8,128)S(1)}, f32[128,4,128]{2,1,0:T(4,128)S(1)}) custom-call(s32[1,128]{1,0:T(1,128)S(1)} %bitcast.1, f32[128,4,512]{2,1,0:T(4,128)} %grad_ref.1, f32[2,128,512]{2,1,0:T(8,128)} %lf_ref.1, f32[2,128,512]{2,1,0:T(8,128)} %rf_ref.1, f32[2,128,512]{2,1,0:T(8,128)} %lroot_ref.1, ...), custom_call_target="tpu_custom_call" | custom-call | flops 1610612736 | bytes 4500000 | tf_op jit(solution)/shard_map/pallas_call | solution.py:375
  77.1 1.1 %shard_map.86 = (f32[2,128,512]{2,1,0:T(8,128)}, f32[2,128,512]{2,1,0:T(8,128)}, f32[128,4,128]{2,1,0:T(4,128)}) custom-call(f32[2,128,512]{2,1,0:T(8,128)S(1)} %get-tuple-element.6.a, f32[2,128,512]{2,1,0:T(8,128)S(1)} %get-tuple-element.7.b, f32[128,4,128]{2,1,0:T(4,128)S(1)} %get-tuple-element.8.c), custom_call_target="tpu_custom_call" | custom-call | tf_op jit(solution)/shard_map/pallas_call | solution.py:423
Async XLA Ops:
  0.6 0.7 copy-start

commit v5 on v4

--- a/solution.py
+++ b/solution.py
@@ -12,8 +12,9 @@
 i32 = jnp.int32
 
 NF, NX = 128, 4
-IN0, IN1, OUT, LA, LB, LFA, LFB = range(7)
-XA0, XA1, XB0, XB1, XFA, XFB = range(6)
+OUT, LA, LB, LC = range(4)
+XA, XB, XC = range(3)
+NQ = 4
 
 
 def split(x):
@@ -33,7 +34,7 @@
     left_out, right_out, dir_out,
     gq, send, gbuf, band, acc, ghi, glo, lown, lbuf, lhi, llo, rr, rhi, rlo, lf, rf, dbuf, rbuf,
     left_new, right_new, dir_new, row_v, tab_v, tab_s,
-    send_sem, recv_sem, x_send_sem, x_recv_sem, loc_sem, in_sem, out_sem,
+    send_sem, recv_sem, p_send_sem, p_recv_sem, x_send_sem, x_recv_sem, loc_sem, in_sem, out_sem,
 ):
     me, r = lax.axis_index("fsdp"), lax.axis_index("rep")
     chip, core = lax.div(me, 2), lax.rem(me, 2)
@@ -66,7 +67,7 @@
             def _():
                 pl.semaphore_signal(barrier, inc=1, device_id=(f, r), device_id_type=MESH)
 
-    for x in (xa, xb):
+    for x in (xa, xb, xc):
         pl.semaphore_signal(barrier, inc=1, device_id=(me, x), device_id_type=MESH)
 
     in_o.wait()
@@ -97,7 +98,7 @@
     def wait_bytes(ref, sem):
         pltpu.make_async_copy(ref, ref, sem).wait()
 
-    to_a, to_b = (me, xa), (me, xb)
+    to_a, to_b, to_c = (me, xa), (me, xb), (me, xc)
 
     to_s.wait()
     in_g.wait()
@@ -108,25 +109,24 @@
             send[k, o] = gq[tab_s[k, o]]
 
     pack(0)
-    pl.semaphore_wait(barrier, NF - 1 + 2)
+    pl.semaphore_wait(barrier, NF - 1 + 3)
 
     def send_in(k, cc):
+        def piece(o, place, h):
+            pltpu.make_async_remote_copy(
+                src_ref=send.at[k, o], dst_ref=gbuf.at[k, r, place],
+                send_sem=p_send_sem.at[k, h], recv_sem=p_recv_sem.at[k, h],
+                device_id=(o, r), device_id_type=MESH,
+            ).start()
+
         @pl.when(core != cc)
         def _():
-            o = chip * 2 + cc
-            remote(send.at[k, o], gbuf.at[k, r, core], IN1, k, (o, r)).start()
-
-        def piece(j, kind):
+            piece(chip * 2 + cc, core, NQ - 1)
+
+        @pl.loop(1, NF // 2)
+        def _(j):
             o = lax.rem(chip + j, NF // 2) * 2 + cc
-            remote(send.at[k, o], gbuf.at[k, r, (NF // 2 - j) * 2 + core], kind, k, (o, r)).start()
-
-        @pl.loop(1, 33, unroll=4)
-        def _(j):
-            piece(j, IN0)
-
-        @pl.loop(33, NF // 2)
-        def _(j):
-            piece(j, IN1)
+            piece(o, (NF // 2 - j) * 2 + core, lax.div(j - 1, 16))
 
     def own_copy(src, dst, i, k):
         c = pltpu.make_async_copy(src, dst, loc_sem.at[i, k])
@@ -149,6 +149,7 @@
             block_to(xc, 2, LA, to_b)
         else:
             block_to(xc, 2, LB, to_a)
+        block_to(r, 5, LC, to_c)
 
     l_start(0)
     send_in(0, 1)
@@ -162,12 +163,6 @@
     from_a = (pl.ds(0, 3), pl.ds(0, 2))
     from_b = (pl.ds(3, 2), pl.ds(2, 3))
 
-    def l_forward(k):
-        wait_bytes(lbuf.at[k, from_a[k]], recv_sem.at[LA, k])
-        remote(lbuf.at[k, 0, pl.ds(0, 64)], lbuf.at[k, 5, pl.ds(0, 64)], LFA, k, to_b).start()
-        wait_bytes(lbuf.at[k, from_b[k]], recv_sem.at[LB, k])
-        remote(lbuf.at[k, 3, pl.ds(64, 64)], lbuf.at[k, 5, pl.ds(64, 64)], LFB, k, to_a).start()
-
     def l_put(k, p, q, x):
         hi, lo = split(x)
         lhi[k, at128(p), at128(q)] = hi
@@ -183,6 +178,10 @@
             l_both(k, r, q, lown[k, :, at128(q)])
 
     def l_take(k):
+        wait_bytes(lbuf.at[k, from_a[k]], recv_sem.at[LA, k])
+        wait_bytes(lbuf.at[k, from_b[k]], recv_sem.at[LB, k])
+        wait_bytes(lbuf.at[k, 5], recv_sem.at[LC, k])
+        l_put(k, xc, xc, lbuf[k, 5])
         l_put(k, xa, xa, lbuf[k, 0])
         l_both(k, xa, xc, lbuf[k, 1])
         if k == 0:
@@ -192,41 +191,22 @@
         l_put(k, xb, xb, lbuf[k, 3])
         l_both(k, xb, xc, lbuf[k, 4])
 
-    def l_end(k):
-        wait_bytes(lbuf.at[k, 5, pl.ds(0, 64)], recv_sem.at[LFA, k])
-        wait_bytes(lbuf.at[k, 5, pl.ds(64, 64)], recv_sem.at[LFB, k])
-        l_put(k, xc, xc, lbuf[k, 5])
-
-    half_at = (64, 0)
-
-    def quarters(k, q, h):
-        return gbuf.at[k, q, pl.ds(half_at[h], 32)], gbuf.at[k, q, pl.ds(half_at[h] + 32, 32)]
-
-    def x_remote(ref, kind, k, h, dev):
-        pltpu.make_async_remote_copy(
-            src_ref=ref, dst_ref=ref, send_sem=x_send_sem.at[kind, k, h], recv_sem=x_recv_sem.at[kind, k, h],
-            device_id=dev, device_id_type=MESH,
-        ).start()
+    def quarter(k, q, h):
+        return gbuf.at[k, q, pl.ds((NQ - 1 - h) * 32, 32)]
+
+    def arrivals(k, h):
+        return gbuf.at[k, r, pl.ds((NQ - 1 - h) * 32, 32 if h < NQ - 1 else 31)]
 
     def x_start(k, h):
-        if h == 0:
-            wait_bytes(gbuf.at[k, r, pl.ds(64, 64)], recv_sem.at[IN0, k])
-        else:
-            wait_bytes(gbuf.at[k, r, pl.ds(0, 63)], recv_sem.at[IN1, k])
+        wait_bytes(arrivals(k, h), p_recv_sem.at[k, h])
+        if h == NQ - 1:
             own_in[k].wait()
-        g0, g1 = quarters(k, r, h)
-        x_remote(g0, XA0, k, h, to_a)
-        x_remote(g1, XB1, k, h, to_b)
-        x_remote(g1, XA1, k, h, to_a)
-        x_remote(g0, XB0, k, h, to_b)
-
-    def x_forward(k, h):
-        g0, _ = quarters(k, xb, h)
-        wait_bytes(g0, x_recv_sem.at[XA0, k, h])
-        x_remote(g0, XFA, k, h, to_a)
-        _, g1 = quarters(k, xa, h)
-        wait_bytes(g1, x_recv_sem.at[XB1, k, h])
-        x_remote(g1, XFB, k, h, to_b)
+        g = quarter(k, r, h)
+        for kind, dev in ((XC, to_c), (XA, to_a), (XB, to_b)):
+            pltpu.make_async_remote_copy(
+                src_ref=g, dst_ref=g, send_sem=x_send_sem.at[kind, k, h], recv_sem=x_recv_sem.at[kind, k, h],
+                device_id=dev, device_id_type=MESH,
+            ).start()
 
     def take(k, q, start=False):
         @pl.loop(0, 8)
@@ -245,27 +225,17 @@
         else:
             acc[...] += part
 
-    def x_take_near(k):
-        for h in range(2):
-            _, g1 = quarters(k, xb, h)
-            wait_bytes(g1, x_recv_sem.at[XA1, k, h])
-        take(k, xb)
-        for h in range(2):
-            g0, _ = quarters(k, xa, h)
-            wait_bytes(g0, x_recv_sem.at[XB0, k, h])
-        take(k, xa)
-
-    def x_take_far(k):
-        for h in range(2):
-            g0, g1 = quarters(k, xc, h)
-            wait_bytes(g0, x_recv_sem.at[XFA, k, h])
-            wait_bytes(g1, x_recv_sem.at[XFB, k, h])
-        take(k, xc)
-
-    def steer_and_send(k):
-        t = split(acc[...])
-
-        @pl.loop(0, 4)
+    def x_take(k):
+        for kind, q in ((XA, xb), (XB, xa), (XC, xc)):
+            for h in range(NQ):
+                wait_bytes(quarter(k, q, h), x_recv_sem.at[kind, k, h])
+            take(k, q)
+
+    def steer(k):
+        return split(acc[...])
+
+    def bands_out(k, t, start, stop):
+        @pl.loop(start, stop)
         def _(i):
             p = lax.rem(lax.div(chip, 16) + i, 4)
             band[pl.ds(0, 128), :] = dot3((lhi[k, at128(p), :], llo[k, at128(p), :]), t, ((1,), (0,)))
@@ -282,6 +252,7 @@
 
             pl.loop(1, 32)(piece)
 
+    def own_piece_out(k):
         return own_copy(dbuf.at[k, me], rbuf.at[k * NF + me], 1, k)
 
     weight = (1.0 - moment_decay) / 512
@@ -300,28 +271,26 @@
     in_r.wait()
     for k in range(2):
         rhi[k], rlo[k] = split(jnp.transpose(rr[k]))
-    l_forward(0)
+    for h in range(NQ - 1):
+        x_start(0, h)
     l_take(0)
-    x_start(0, 0)
-    x_start(0, 1)
+    x_start(0, NQ - 1)
     take(0, r, True)
-    x_forward(0, 0)
-    l_forward(1)
-    x_forward(0, 1)
-    l_end(0)
-    x_take_near(0)
+    x_take(0)
+    t = steer(0)
+    bands_out(0, t, 0, 2)
     x_start(1, 0)
-    x_take_far(0)
-    own_out0 = steer_and_send(0)
+    bands_out(0, t, 2, 4)
+    own_out0 = own_piece_out(0)
     x_start(1, 1)
-    x_forward(1, 0)
+    l_take(1)
+    for h in range(2, NQ):
+        x_start(1, h)
     take(1, r, True)
-    x_forward(1, 1)
-    l_take(1)
-    l_end(1)
-    x_take_near(1)
-    x_take_far(1)
-    own_out1 = steer_and_send(1)
+    x_take(1)
+    t = steer(1)
+    bands_out(1, t, 0, 4)
+    own_out1 = own_piece_out(1)
     in_lf.wait()
     in_rf.wait()
     stats(0)
@@ -343,16 +312,14 @@
     out_d = pltpu.make_async_copy(dir_new, dir_out, out_sem.at[2])
     out_d.start()
     for k in range(2):
-        wait_bytes(gbuf.at[k, r, pl.ds(64, 64)], send_sem.at[IN0, k])
-        wait_bytes(gbuf.at[k, r, pl.ds(0, 63)], send_sem.at[IN1, k])
+        for h in range(NQ):
+            wait_bytes(arrivals(k, h), p_send_sem.at[k, h])
+            for kind in (XA, XB, XC):
+                wait_bytes(quarter(k, r, h), x_send_sem.at[kind, k, h])
         wait_bytes(rbuf.at[pl.ds(k * NF, NF - 1)], send_sem.at[OUT, k])
-        for kind in (XA0, XA1, XB0, XB1, XFA, XFB):
-            for h in range(2):
-                wait_bytes(gbuf.at[k, r, pl.ds(0, 32)], x_send_sem.at[kind, k, h])
         wait_bytes(lbuf.at[k, from_a[k]], send_sem.at[LA, k])
         wait_bytes(lbuf.at[k, from_b[k]], send_sem.at[LB, k])
-        for kind in (LFA, LFB):
-            wait_bytes(lbuf.at[k, 5, pl.ds(0, 64)], send_sem.at[kind, k])
+        wait_bytes(lbuf.at[k, 5], send_sem.at[LC, k])
     out_l.wait()
     out_r.wait()
     out_d.wait()
@@ -406,10 +373,12 @@
             pltpu.VMEM((1, 128), i32),
             pltpu.VMEM((8, 128), i32),
             pltpu.SMEM((8, 128), i32),
-            pltpu.SemaphoreType.DMA((7, 2)),
-            pltpu.SemaphoreType.DMA((7, 2)),
-            pltpu.SemaphoreType.DMA((6, 2, 2)),
-            pltpu.SemaphoreType.DMA((6, 2, 2)),
+            pltpu.SemaphoreType.DMA((4, 2)),
+            pltpu.SemaphoreType.DMA((4, 2)),
+            pltpu.SemaphoreType.DMA((2, NQ)),
+            pltpu.SemaphoreType.DMA((2, NQ)),
+            pltpu.SemaphoreType.DMA((3, 2, NQ)),
+            pltpu.SemaphoreType.DMA((3, 2, NQ)),
             pltpu.SemaphoreType.DMA((3, 2)),
             pltpu.SemaphoreType.DMA((6,)),
             pltpu.SemaphoreType.DMA((3,)),

time: 78.3 us -> 80.4 us (1.027)
  Pallas kernels: 76.9 us -> 79 us
    pallas_call x1, Pallas kernels: 75.8 us -> 77.9 us  [body(): pl.pallas_call(kernel, out_shape=(jax.ShapeDtypeStruct((2, 128, 512), f32...]
where the time goes in v5:
time: 80.4 us; the launch traced here: 80.3 us
  Pallas kernels  79 us (98%)
    pallas_call x1, Pallas kernels, body(): pl.pallas_call(kernel, out_shape=(jax.ShapeDtypeStruct((2, 128, 512), f32...  77.9 us

profile of v5, /device:TPU:1, one launch (start us, length us, event | category | flops | bytes accessed | tf_op | source)
XLA Modules:
  0.0 80.3 jit_solution(11034629680301511008)
XLA Ops:
  0.6 0.0 copy-start
  0.6 0.6 copy-done
  1.3 77.9 %shard_map.85 = (f32[2,128,512]{2,1,0:T(8,128)S(1)}, f32[2,128,512]{2,1,0:T(8,128)S(1)}, f32[128,4,128]{2,1,0:T(4,128)S(1)}) custom-call(s32[1,128]{1,0:T(1,128)S(1)} %bitcast.1, f32[128,4,512]{2,1,0:T(4,128)} %grad_ref.1, f32[2,128,512]{2,1,0:T(8,128)} %lf_ref.1, f32[2,128,512]{2,1,0:T(8,128)} %rf_ref.1, f32[2,128,512]{2,1,0:T(8,128)} %lroot_ref.1, ...), custom_call_target="tpu_custom_call" | custom-call | flops 1610612736 | bytes 4500000 | tf_op jit(solution)/shard_map/pallas_call | solution.py:342
  79.2 1.1 %shard_map.86 = (f32[2,128,512]{2,1,0:T(8,128)}, f32[2,128,512]{2,1,0:T(8,128)}, f32[128,4,128]{2,1,0:T(4,128)}) custom-call(f32[2,128,512]{2,1,0:T(8,128)S(1)} %get-tuple-element.6.a, f32[2,128,512]{2,1,0:T(8,128)S(1)} %get-tuple-element.7.b, f32[128,4,128]{2,1,0:T(4,128)S(1)} %get-tuple-element.8.c), custom_call_target="tpu_custom_call" | custom-call | tf_op jit(solution)/shard_map/pallas_call | solution.py:392
Async XLA Ops:
  0.6 0.7 copy-start

commit v6 on v4

--- a/solution.py
+++ b/solution.py
@@ -33,11 +33,14 @@
     left_out, right_out, dir_out,
     gq, send, gbuf, band, acc, ghi, glo, lown, lbuf, lhi, llo, rr, rhi, rlo, lf, rf, dbuf, rbuf,
     left_new, right_new, dir_new, row_v, tab_v, tab_s,
-    send_sem, recv_sem, x_send_sem, x_recv_sem, loc_sem, in_sem, out_sem,
+    send_sem, recv_sem, in_send_sem, x_send_sem, x_recv_sem, loc_sem, in_sem, out_sem,
 ):
     me, r = lax.axis_index("fsdp"), lax.axis_index("rep")
     chip, core = lax.div(me, 2), lax.rem(me, 2)
     xa, xb, xc = lax.rem(r + 1, NX), lax.rem(r + 3, NX), lax.rem(r + 2, NX)
+
+    def far_first(i):
+        return NF // 4 + lax.div(i + 1, 2) * (1 - 2 * lax.rem(i, 2))
 
     def at128(q):
         return pl.ds(pl.multiple_of(q * 128, 128), 128)
@@ -111,22 +114,30 @@
     pl.semaphore_wait(barrier, NF - 1 + 2)
 
     def send_in(k, cc):
+        def piece(o, place, kind, sem):
+            pltpu.make_async_remote_copy(
+                src_ref=send.at[k, o], dst_ref=gbuf.at[k, r, place], send_sem=sem, recv_sem=recv_sem.at[kind, k],
+                device_id=(o, r), device_id_type=MESH,
+            ).start()
+
         @pl.when(core != cc)
         def _():
-            o = chip * 2 + cc
-            remote(send.at[k, o], gbuf.at[k, r, core], IN1, k, (o, r)).start()
-
-        def piece(j, kind):
-            o = lax.rem(chip + j, NF // 2) * 2 + cc
-            remote(send.at[k, o], gbuf.at[k, r, (NF // 2 - j) * 2 + core], kind, k, (o, r)).start()
-
-        @pl.loop(1, 33, unroll=4)
-        def _(j):
-            piece(j, IN0)
-
-        @pl.loop(33, NF // 2)
-        def _(j):
-            piece(j, IN1)
+            piece(chip * 2 + cc, core, IN1, in_send_sem.at[k, 2, 0])
+
+        def piece_to(i, kind, h):
+            o = lax.rem(chip + far_first(i), NF // 2) * 2 + cc
+            piece(o, (NF // 2 - 1 - i) * 2 + core, kind, in_send_sem.at[k, cc, h])
+
+        @pl.loop(0, 32, unroll=4)
+        def _(i):
+            piece_to(i, IN0, 0)
+
+        @pl.loop(32, NF // 2 - 1)
+        def _(i):
+            piece_to(i, IN1, 1)
+
+    def in_sent(k, cc, h):
+        wait_bytes(send.at[k, pl.ds(0, 32 - h)], in_send_sem.at[k, cc, h])
 
     def own_copy(src, dst, i, k):
         c = pltpu.make_async_copy(src, dst, loc_sem.at[i, k])
@@ -134,8 +145,6 @@
         return c
 
     own_in = [None, None]
-    send_in(0, 0)
-    in_l.wait()
 
     def l_start(k):
         def block_to(q, slot, kind, dev):
@@ -149,15 +158,6 @@
             block_to(xc, 2, LA, to_b)
         else:
             block_to(xc, 2, LB, to_a)
-
-    l_start(0)
-    send_in(0, 1)
-    own_in[0] = own_copy(send.at[0, me], gbuf.at[0, r, core], 0, 0)
-    l_start(1)
-    pack(1)
-    send_in(1, 0)
-    send_in(1, 1)
-    own_in[1] = own_copy(send.at[1, me], gbuf.at[1, r, core], 0, 1)
 
     from_a = (pl.ds(0, 3), pl.ds(0, 2))
     from_b = (pl.ds(3, 2), pl.ds(2, 3))
@@ -233,7 +233,8 @@
         def _(i):
             for j in range(8):
                 m = i * 8 + j
-                base = pl.multiple_of(lax.rem(chip + m, NF // 2) * 8, 8)
+                source = lax.rem(chip + NF // 2 - far_first(NF // 2 - 1 - m), NF // 2)
+                base = pl.multiple_of(source * 8, 8)
                 band[pl.ds(base, 4), :] = gbuf[k, q, 2 * m]
                 band[pl.ds(base + 4, 4), :] = gbuf[k, q, 2 * m + 1]
 
@@ -266,21 +267,24 @@
         t = split(acc[...])
 
         @pl.loop(0, 4)
+        def _(p):
+            band[at128(p), :] = dot3((lhi[k, at128(p), :], llo[k, at128(p), :]), t, ((1,), (0,)))
+
+        @pl.loop(0, NF // 8)
         def _(i):
-            p = lax.rem(lax.div(chip, 16) + i, 4)
-            band[pl.ds(0, 128), :] = dot3((lhi[k, at128(p), :], llo[k, at128(p), :]), t, ((1,), (0,)))
-            for j in range(32):
-                dbuf[k, p * 32 + j] = band[pl.ds(j * 4, 4), :]
-
-            def piece(j):
-                f = p * 32 + lax.rem(me + j, 32)
-                remote(dbuf.at[k, f], rbuf.at[k * NF + me], OUT, k, (f, r)).start()
-
-            @pl.when(i > 0)
-            def _():
-                piece(0)
-
-            pl.loop(1, 32)(piece)
+            for j in range(8):
+                dbuf[k, i * 8 + j] = band[pl.ds(pl.multiple_of(i * 32, 32) + j * 4, 4), :]
+
+        def piece(f):
+            remote(dbuf.at[k, f], rbuf.at[k * NF + me], OUT, k, (f, r)).start()
+
+        @pl.loop(0, NF // 2 - 1)
+        def _(i):
+            f = lax.rem(chip + far_first(i), NF // 2) * 2
+            piece(f)
+            piece(f + 1)
+
+        piece(chip * 2 + 1 - core)
 
         return own_copy(dbuf.at[k, me], rbuf.at[k * NF + me], 1, k)
 
@@ -295,6 +299,15 @@
         old = rf[k]
         right_new[k] = jnp.where(live[k] > 0, moment_decay * old + weight * term, old)
 
+    send_in(0, 0)
+    own_in[0] = own_copy(send.at[0, me], gbuf.at[0, r, core], 0, 0)
+    in_l.wait()
+    l_start(0)
+    send_in(0, 1)
+    pack(1)
+    own_in[1] = own_copy(send.at[1, me], gbuf.at[1, r, core], 0, 1)
+    send_in(1, 0)
+    send_in(1, 1)
     l_own(0)
     l_own(1)
     in_r.wait()
@@ -306,15 +319,16 @@
     x_start(0, 1)
     take(0, r, True)
     x_forward(0, 0)
-    l_forward(1)
     x_forward(0, 1)
+    l_start(1)
     l_end(0)
     x_take_near(0)
-    x_start(1, 0)
     x_take_far(0)
     own_out0 = steer_and_send(0)
+    x_start(1, 0)
     x_start(1, 1)
     x_forward(1, 0)
+    l_forward(1)
     take(1, r, True)
     x_forward(1, 1)
     l_take(1)
@@ -343,8 +357,10 @@
     out_d = pltpu.make_async_copy(dir_new, dir_out, out_sem.at[2])
     out_d.start()
     for k in range(2):
-        wait_bytes(gbuf.at[k, r, pl.ds(64, 64)], send_sem.at[IN0, k])
-        wait_bytes(gbuf.at[k, r, pl.ds(0, 63)], send_sem.at[IN1, k])
+        wait_bytes(send.at[k, 0], in_send_sem.at[k, 2, 0])
+        for cc in range(2):
+            for h in range(2):
+                in_sent(k, cc, h)
         wait_bytes(rbuf.at[pl.ds(k * NF, NF - 1)], send_sem.at[OUT, k])
         for kind in (XA0, XA1, XB0, XB1, XFA, XFB):
             for h in range(2):
@@ -408,6 +424,7 @@
             pltpu.SMEM((8, 128), i32),
             pltpu.SemaphoreType.DMA((7, 2)),
             pltpu.SemaphoreType.DMA((7, 2)),
+            pltpu.SemaphoreType.DMA((2, 3, 2)),
             pltpu.SemaphoreType.DMA((6, 2, 2)),
             pltpu.SemaphoreType.DMA((6, 2, 2)),
             pltpu.SemaphoreType.DMA((3, 2)),

time: 78.3 us -> 74.6 us (0.953)
  Pallas kernels: 76.9 us -> 73.2 us
    pallas_call x1, Pallas kernels: 75.8 us -> 72.1 us  [body(): pl.pallas_call(kernel, out_shape=(jax.ShapeDtypeStruct((2, 128, 512), f32...]
where the time goes in v6:
time: 74.6 us; the launch traced here: 74.5 us
  Pallas kernels  73.2 us (98%)
    pallas_call x1, Pallas kernels, body(): pl.pallas_call(kernel, out_shape=(jax.ShapeDtypeStruct((2, 128, 512), f32...  72.1 us

profile of v6, /device:TPU:1, one launch (start us, length us, event | category | flops | bytes accessed | tf_op | source)
XLA Modules:
  0.0 74.5 jit_solution(16460627335586914687)
XLA Ops:
  0.6 0.0 copy-start
  0.6 0.6 copy-done
  1.3 72.1 %shard_map.85 = (f32[2,128,512]{2,1,0:T(8,128)S(1)}, f32[2,128,512]{2,1,0:T(8,128)S(1)}, f32[128,4,128]{2,1,0:T(4,128)S(1)}) custom-call(s32[1,128]{1,0:T(1,128)S(1)} %bitcast.1, f32[128,4,512]{2,1,0:T(4,128)} %grad_ref.1, f32[2,128,512]{2,1,0:T(8,128)} %lf_ref.1, f32[2,128,512]{2,1,0:T(8,128)} %rf_ref.1, f32[2,128,512]{2,1,0:T(8,128)} %lroot_ref.1, ...), custom_call_target="tpu_custom_call" | custom-call | flops 1610612736 | bytes 4500000 | tf_op jit(solution)/shard_map/pallas_call | solution.py:391
  73.4 1.1 %shard_map.86 = (f32[2,128,512]{2,1,0:T(8,128)}, f32[2,128,512]{2,1,0:T(8,128)}, f32[128,4,128]{2,1,0:T(4,128)}) custom-call(f32[2,128,512]{2,1,0:T(8,128)S(1)} %get-tuple-element.6.a, f32[2,128,512]{2,1,0:T(8,128)S(1)} %get-tuple-element.7.b, f32[128,4,128]{2,1,0:T(4,128)S(1)} %get-tuple-element.8.c), custom_call_target="tpu_custom_call" | custom-call | tf_op jit(solution)/shard_map/pallas_call | solution.py:440
Async XLA Ops:
  0.6 0.7 copy-start

commit v7 on v6

--- a/solution.py
+++ b/solution.py
@@ -231,12 +231,12 @@
     def take(k, q, start=False):
         @pl.loop(0, 8)
         def _(i):
-            for j in range(8):
-                m = i * 8 + j
-                source = lax.rem(chip + NF // 2 - far_first(NF // 2 - 1 - m), NF // 2)
-                base = pl.multiple_of(source * 8, 8)
-                band[pl.ds(base, 4), :] = gbuf[k, q, 2 * m]
-                band[pl.ds(base + 4, 4), :] = gbuf[k, q, 2 * m + 1]
+            for j in range(4):
+                n = i * 4 + j
+                for m, source in ((2 * n, chip + NF // 2 - n), (2 * n + 1, chip + 1 + n)):
+                    base = pl.multiple_of(lax.rem(source, NF // 2) * 8, 8)
+                    band[pl.ds(base, 4), :] = gbuf[k, q, 2 * m]
+                    band[pl.ds(base + 4, 4), :] = gbuf[k, q, 2 * m + 1]
 
         g = split(band[...])
         ghi[k, :, at128(q)], glo[k, :, at128(q)] = g

time: 74.6 us -> 74.4 us (level)
  no operation moved by 1% of the time
where the time goes in v7:
time: 74.4 us; the launch traced here: 74.2 us
  Pallas kernels  72.9 us (98%)
    pallas_call x1, Pallas kernels, body(): pl.pallas_call(kernel, out_shape=(jax.ShapeDtypeStruct((2, 128, 512), f32...  71.9 us

profile of v7, /device:TPU:1, one launch (start us, length us, event | category | flops | bytes accessed | tf_op | source)
XLA Modules:
  0.0 74.2 jit_solution(13809366055928145195)
XLA Ops:
  0.6 0.0 copy-start
  0.6 0.6 copy-done
  1.3 71.9 %shard_map.85 = (f32[2,128,512]{2,1,0:T(8,128)S(1)}, f32[2,128,512]{2,1,0:T(8,128)S(1)}, f32[128,4,128]{2,1,0:T(4,128)S(1)}) custom-call(s32[1,128]{1,0:T(1,128)S(1)} %bitcast.1, f32[128,4,512]{2,1,0:T(4,128)} %grad_ref.1, f32[2,128,512]{2,1,0:T(8,128)} %lf_ref.1, f32[2,128,512]{2,1,0:T(8,128)} %rf_ref.1, f32[2,128,512]{2,1,0:T(8,128)} %lroot_ref.1, ...), custom_call_target="tpu_custom_call" | custom-call | flops 1610612736 | bytes 4500000 | tf_op jit(solution)/shard_map/pallas_call | solution.py:391
  73.1 1.1 %shard_map.86 = (f32[2,128,512]{2,1,0:T(8,128)}, f32[2,128,512]{2,1,0:T(8,128)}, f32[128,4,128]{2,1,0:T(4,128)}) custom-call(f32[2,128,512]{2,1,0:T(8,128)S(1)} %get-tuple-element.6.a, f32[2,128,512]{2,1,0:T(8,128)S(1)} %get-tuple-element.7.b, f32[128,4,128]{2,1,0:T(4,128)S(1)} %get-tuple-element.8.c), custom_call_target="tpu_custom_call" | custom-call | tf_op jit(solution)/shard_map/pallas_call | solution.py:440
Async XLA Ops:
  0.6 0.7 copy-start
